TPU v7x, 512 devices: a whole 4x8x8 slice. The times are simulated.
512 devices in a mesh: dp: 128 (over z, x, y_hi), rep: 4 (over y_lo, core).
Axes of the slice: x: 4, y: 8 (y_hi: 4, y_lo: 2; y = y_hi * 2 + y_lo), z: 8, core: 2. Of those that a mesh axis runs over, the one named last changes fastest.
Arguments:
- projections: float32 [32768, 256], P('dp'), may hold values from -7 to 7
- partner: int32 [32768], P('dp'), may hold values from 0 to 32767, as said below
- cotangent: float32 [32768], P('dp'), may hold values from 0.3 to 3
Outputs:
- row_loss: float32 [32768], P('dp')
- grad_projections: float32 [32768, 256], P('dp')
Inputs may be any that keep to these rules, and one draw needn't show every extreme that they name: partner[partner[i]] = i and partner[i] != i for every view i.
All inputs are finite; a program needn't handle non-finite values.
Results may differ from a plain program's by a relative error of at most 0.0003.
Values sent between devices are 32-bit elements; how exact they have to be, the bound alone decides.
No kernel may reach another device: no remote copies, remote signals or barrier semaphores. Data moves between devices by JAX's collectives and lax.ppermute only.
A program may use at most 64 MiB of HBM per device.

v0:
```python
import jax
import jax.numpy as jnp
from jax import lax
from jax.sharding import PartitionSpec as P

inv_temp = 10.0
epsilon = 1e-06
highest = lax.Precision.HIGHEST


def passed_along(array, axis, by):
    length = lax.axis_size(axis)
    return lax.ppermute(array, axis, [(i, (i + by) % length) for i in range(length)])


def scores_of(seen_rows, unit_rows):
    return inv_temp * lax.dot_general(
        seen_rows,
        unit_rows,
        (((1,), (1,)), ((), ())),
        precision=highest,
        preferred_element_type=jnp.float32,
    )


def travel(visitor, seen_stats, own_acc, turn_step, turn_count):

    def one_turn(turn_index, carried):
        visitor, seen_stats, own_acc = turn_step(turn_index, carried[0], carried[1], carried[2])
        visitor, seen_stats = passed_along((visitor, seen_stats), "dp", 1)
        return (visitor, seen_stats, own_acc)

    carried = lax.fori_loop(0, turn_count - 1, one_turn, (visitor, seen_stats, own_acc))
    return turn_step(jnp.int32(turn_count - 1), carried[0], carried[1], carried[2])


def send_home(payload, steps_back):
    return passed_along(payload, "dp", -steps_back)


def combine(payload):
    return lax.psum(payload, "rep")


def by_loop(unit_rows, partner, cotangent):
    own_count = unit_rows.shape[0]
    cycle_size = lax.axis_size("dp")
    group_size = lax.axis_size("rep")
    cycle_place = lax.axis_index("dp")
    member = lax.axis_index("rep")
    half_cycle = cycle_size // 2
    own_ids = cycle_place * own_count + jnp.arange(own_count, dtype=jnp.int32)
    seen_count = own_count // group_size
    seen_first = member * seen_count
    turn_count = half_cycle + 1
    start_block = lax.dynamic_slice_in_dim(unit_rows, seen_first, seen_count, 0)
    seen_positions = jnp.arange(seen_count, dtype=jnp.int32)
    steps_back = turn_count - 1

    def visit_of(turn_index):
        source = (cycle_place - turn_index) % cycle_size
        seen_ids = source * own_count + seen_first + seen_positions
        row_weight = (turn_index <= half_cycle).astype(jnp.float32)
        col_weight = jnp.logical_and(turn_index >= 1, turn_index < half_cycle).astype(jnp.float32)
        notself = (seen_ids[:, None] != own_ids[None, :]).astype(jnp.float32)
        paired = (partner[None, :] == seen_ids[:, None]).astype(jnp.float32)
        return (row_weight, col_weight, notself, paired)

    def sum_turn(turn_index, visitor, seen_stats, own_acc):
        row_weight, col_weight, notself, paired = visit_of(turn_index)
        scores = scores_of(visitor[0], unit_rows)
        exp_scores = jnp.exp(scores) * notself
        hit_scores = scores * paired
        own_acc = own_acc + row_weight * jnp.stack(
            [jnp.sum(exp_scores, axis=0), jnp.sum(hit_scores, axis=0)]
        )
        seen_stats = seen_stats + col_weight * jnp.stack(
            [jnp.sum(exp_scores, axis=1), jnp.sum(hit_scores, axis=1)]
        )
        return (visitor, seen_stats, own_acc)

    first_trip = travel(
        start_block[None],
        jnp.zeros((2, seen_count), jnp.float32),
        jnp.zeros((2, own_count), jnp.float32),
        sum_turn,
        turn_count,
    )
    returned = send_home(first_trip[1], steps_back)
    placed = lax.dynamic_update_slice_in_dim(
        jnp.zeros((2, own_count), jnp.float32), returned, seen_first, 1
    )
    totals = combine(first_trip[2] + placed)
    log_sums = jnp.log(totals[0])
    row_loss = log_sums - totals[1]
    own_pair = jnp.stack([log_sums, cotangent])
    seen_pair = lax.dynamic_slice_in_dim(own_pair, seen_first, seen_count, 1)

    def grad_turn(turn_index, visitor, seen_pair, own_acc):
        row_weight, col_weight, notself, paired = visit_of(turn_index)
        seen_rows = visitor[0]
        scores = scores_of(seen_rows, unit_rows)
        own_part = jnp.exp(scores - log_sums[None, :]) * notself
        seen_part = jnp.exp(scores - seen_pair[0][:, None]) * notself
        pair_weights = cotangent[None, :] * (own_part - paired) + seen_pair[1][:, None] * (
            seen_part - paired
        )
        own_term = lax.dot_general(
            pair_weights,
            seen_rows,
            (((0,), (0,)), ((), ())),
            precision=highest,
            preferred_element_type=jnp.float32,
        )
        own_acc = own_acc + row_weight * own_term
        seen_term = jnp.dot(
            pair_weights, unit_rows, precision=highest, preferred_element_type=jnp.float32
        )
        seen_grad = visitor[1] + col_weight * seen_term
        return (jnp.stack([seen_rows, seen_grad]), seen_pair, own_acc)

    second_trip = travel(
        jnp.stack([start_block, jnp.zeros_like(start_block)]),
        seen_pair,
        jnp.zeros_like(unit_rows),
        grad_turn,
        turn_count,
    )
    returned_grad = send_home(second_trip[0][1], steps_back)
    placed_grad = lax.dynamic_update_slice_in_dim(
        jnp.zeros_like(unit_rows), returned_grad, seen_first, 0
    )
    unit_grad = inv_temp * combine(second_trip[2] + placed_grad)
    return (row_loss, unit_grad)


def per_device(projections, partner, cotangent):
    row_norms = jnp.sqrt(jnp.sum(projections * projections, axis=1) + epsilon)
    unit_rows = projections / row_norms[:, None]
    row_loss, unit_grad = by_loop(unit_rows, partner, cotangent)
    along = jnp.sum(unit_rows * unit_grad, axis=1)
    grad_projections = (unit_grad - unit_rows * along[:, None]) / row_norms[:, None]
    return (row_loss, grad_projections)


def solution(mesh):
    return jax.shard_map(
        per_device,
        mesh=mesh,
        in_specs=(P("dp", None), P("dp"), P("dp")),
        out_specs=(P("dp"), P("dp", None)),
        check_vma=False,
    )
```

profile of v0, /device:TPU:1, one launch (start us, length us, event | category | flops | bytes accessed | tf_op | source)
XLA Modules:
  0.0 2047.6 jit_solution(14985581304157307757)
XLA Ops:
  9.2 851.6 %while.40 = (s32[]{:T(128)}, f32[1,64,256]{2,1,0:T(8,128)S(1)}, f32[2,64]{1,0:T(2,128)S(1)}, f32[2,256]{1,0:T(2,128)S(1)}, s32[]{:T(128)}, /*index=5*/s32[]{:T(1...) while((s32[]{:T(128)}, f32[1,64,256]{2,1,0:T(8,128)S(1)}, ...), condition=%wide.region_6.7_spmd.clone, body=%wide.region_1.6_spmd.clone.sunk | while | flops 50481232 | bytes 737188 | solution.py:33
  20.3 9.8 collective-permute-done.1
  869.9 77.9 %psum.14 = f32[2,256]{1,0:T(2,128)S(1)} all-reduce(f32[2,256]{1,0:T(2,128)S(1)} %add.261), channel_id=1, replica_groups=mesh['dp'=128,'rep'=4] {'rep'}, use_global_device_ids=true, to_apply=%region_11.12 | all-reduce | flops 512 | bytes 4096 | tf_op jit(solution)/shard_map/psum | solution.py:42
  948.6 1014.0 %while.41 = (s32[]{:T(128)}, f32[2,64,256]{2,1,0:T(8,128)S(1)}, f32[2,64]{1,0:T(2,128)S(1)}, f32[256,256]{1,0:T(8,128)S(1)}, f32[256]{0:T(256)S(1)}, /*index=5*/...) while((s32[]{:T(128)}, f32[2,64,256]{2,1,0:T(8,128)S(1)}, ...), condition=%wide.region_13.14_spmd.clone, body=%wide.region_12.13_spmd.clone.sunk | while | flops 151470416 | bytes 2698420 | solution.py:33
  953.8 10.2 collective-permute-done.2
  969.2 9.6 collective-permute-done.2
  1058.0 10.3 collective-permute-done.2
  1073.6 10.8 collective-permute-done.2
  1089.6 9.9 collective-permute-done.2
  1104.7 10.3 collective-permute-done.2
  1120.3 10.8 collective-permute-done.2
  1136.3 10.7 collective-permute-done.2
  1152.3 10.8 collective-permute-done.2
  1168.3 10.8 collective-permute-done.2
  1184.3 10.8 collective-permute-done.2
  1200.4 10.8 collective-permute-done.2
  1216.4 10.8 collective-permute-done.2
  1232.4 10.8 collective-permute-done.2
  1248.4 10.8 collective-permute-done.2
  1264.4 10.8 collective-permute-done.2
  1280.4 10.8 collective-permute-done.2
  1296.5 10.8 collective-permute-done.2
  1312.5 10.8 collective-permute-done.2
  1328.5 10.8 collective-permute-done.2
  1344.5 10.8 collective-permute-done.2
  1360.5 10.8 collective-permute-done.2
  1376.5 10.8 collective-permute-done.2
  1392.5 10.8 collective-permute-done.2
  1408.5 10.8 collective-permute-done.2
  1424.5 10.8 collective-permute-done.2
  1440.5 10.8 collective-permute-done.2
  1456.5 10.8 collective-permute-done.2
  1472.5 10.8 collective-permute-done.2
  1488.5 10.8 collective-permute-done.2
  1504.5 10.8 collective-permute-done.2
  1520.5 10.7 collective-permute-done.2
  1536.5 10.8 collective-permute-done.2
  1552.5 10.7 collective-permute-done.2
  1568.4 10.7 collective-permute-done.2
  1584.4 10.7 collective-permute-done.2
  1600.4 10.7 collective-permute-done.2
  1616.3 10.7 collective-permute-done.2
  1632.3 10.7 collective-permute-done.2
  1648.2 10.7 collective-permute-done.2
  1664.2 10.7 collective-permute-done.2
  1680.1 10.7 collective-permute-done.2
  1696.1 10.7 collective-permute-done.2
  1712.0 10.7 collective-permute-done.2
  1727.9 10.7 collective-permute-done.2
  1743.9 10.7 collective-permute-done.2
  1759.8 10.7 collective-permute-done.2
  1775.7 10.7 collective-permute-done.2
  1791.7 10.8 collective-permute-done.2
  1807.7 10.8 collective-permute-done.2
  1823.7 10.8 collective-permute-done.2
  1839.8 10.4 collective-permute-done.2
  1855.4 10.7 collective-permute-done.2
  1871.4 10.7 collective-permute-done.2
  1887.3 11.0 collective-permute-done.2
  1903.6 10.4 collective-permute-done.2
  1919.2 10.7 collective-permute-done.2
  1935.2 10.7 collective-permute-done.2
  1951.1 11.4 collective-permute-done.2
  1974.3 64.4 %all-reduce.3.cloned.1.call-done = f32[256,256]{1,0:T(8,128)} async-done(((f32[256,256]{1,0:T(8,128)}), f32[256,256]{1,0:T(8,128)}) %all-reduce.3.cloned.1.call-update) | async-done | bytes 262160 | tf_op jit(solution)/shard_map/psum | solution.py:42
  (1518 shorter events, 1234.3 us)
Async XLA Ops:
  7.2 2031.5 %all-reduce.3.cloned.1.call-start = ((), (), s32[]{:S(2)}) async-start(), calls=%async_computation | async-start | bytes 524288 | tf_op jit(solution)/shard_map/psum | solution.py:42
  9.2 20.9 %collective-permute-start = (f32[1,64,256]{2,1,0:T(8,128)S(1)}, f32[1,64,256]{2,1,0:T(8,128)S(1)}, u32[]{:S(2)}, u32[]{:S(2)}) collective-permute-start(f32[1,64,256]{2,1,0:T(8,128)S(1)} %copy.10), channel_id=1, source_target_pairs={{0,4},{4,8},{8,12},{12,16},{16,20},{20,24},{24,28},{28,32},{32,36}... | collective-permute-start | bytes 196616 | tf_op jit(solution)/shard_map/while/body/eval_jaxpr/ppermute | solution.py:13
  14.8 15.3 collective-permute-start.1
  948.6 15.4 collective-permute-start.3
  964.0 14.8 collective-permute-start.3
  978.8 14.8 collective-permute-start.3
  1023.2 14.8 collective-permute-start.3
  1052.8 15.5 collective-permute-start.3
  1068.4 16.0 collective-permute-start.3
  1084.4 15.1 collective-permute-start.3
  1099.6 15.5 collective-permute-start.3
  1115.1 16.0 collective-permute-start.3
  1131.1 15.9 collective-permute-start.3
  1147.1 16.0 collective-permute-start.3
  1163.2 16.0 collective-permute-start.3
  1179.2 16.0 collective-permute-start.3
  1195.2 16.0 collective-permute-start.3
  1211.2 16.0 collective-permute-start.3
  1227.2 16.0 collective-permute-start.3
  1243.2 16.0 collective-permute-start.3
  1259.3 16.0 collective-permute-start.3
  1275.3 16.0 collective-permute-start.3
  1291.3 16.0 collective-permute-start.3
  1307.3 16.0 collective-permute-start.3
  1323.3 16.0 collective-permute-start.3
  1339.3 16.0 collective-permute-start.3
  1355.3 16.0 collective-permute-start.3
  1371.3 16.0 collective-permute-start.3
  1387.4 16.0 collective-permute-start.3
  1403.3 16.0 collective-permute-start.3
  1419.4 16.0 collective-permute-start.3
  1435.3 16.0 collective-permute-start.3
  1451.4 16.0 collective-permute-start.3
  1467.3 16.0 collective-permute-start.3
  1483.3 16.0 collective-permute-start.3
  1499.3 16.0 collective-permute-start.3
  1515.3 15.9 collective-permute-start.3
  1531.3 15.9 collective-permute-start.3
  1547.3 15.9 collective-permute-start.3
  1563.2 15.9 collective-permute-start.3
  1579.2 15.9 collective-permute-start.3
  1595.2 15.9 collective-permute-start.3
  1611.2 15.9 collective-permute-start.3
  1627.1 15.9 collective-permute-start.3
  1643.1 15.9 collective-permute-start.3
  1659.0 15.9 collective-permute-start.3
  1674.9 15.9 collective-permute-start.3
  1690.9 15.9 collective-permute-start.3
  1706.8 15.9 collective-permute-start.3
  1722.8 15.9 collective-permute-start.3
  1738.7 15.9 collective-permute-start.3
  1754.6 15.9 collective-permute-start.3
  1770.6 15.9 collective-permute-start.3
  1786.5 16.0 collective-permute-start.3
  1802.5 16.0 collective-permute-start.3
  1818.6 16.0 collective-permute-start.3
  1834.6 15.6 collective-permute-start.3
  1850.3 15.9 collective-permute-start.3
  1866.2 15.9 collective-permute-start.3
  1882.2 16.2 collective-permute-start.3
  1898.4 15.6 collective-permute-start.3
  1914.0 15.9 collective-permute-start.3
  1930.0 15.9 collective-permute-start.3
  1945.9 16.6 collective-permute-start.3
  (200 other events, 2407.9 us)
Sparse Core Ops, SparseCore 0:
  1973.9 64.7 all-reduce.2
where the time goes:
time: 2050 us
  waiting for transfers between devices  1310 us (64%)
  starting transfers between devices  512 us (25%)
  matrix products  109 us (5%)
  blocking collectives  77.9 us (4%)
    ppermute x258, waiting for transfers between devices, passed_along(): lax.ppermute(array, axis, [(i, (i + by) % length) for i in range(length)])  1240 us
    ppermute x258, starting transfers between devices, passed_along(): lax.ppermute(array, axis, [(i, (i + by) % length) for i in range(length)])  512 us
    psum x1, blocking collectives, combine(): return lax.psum(payload, 'rep')  77.9 us
    psum x1, waiting for transfers between devices, combine(): return lax.psum(payload, 'rep')  64.4 us
    dot_general x130, matrix products, scores_of(): lax.dot_general(seen_rows, unit_rows, (((1,), (1,)), ((), ())), precision...  57.6 us
  transfers between devices with their start and end apart: 259, of which 131 were waited for; matrix products, arithmetic and copies ran while one was open for 6% of the time, Pallas kernels for 0%

commit v1 on v0

v1 whole, which is shorter than its diff:
```python
import functools

import jax
import jax.numpy as jnp
from jax import lax
from jax.experimental import pallas as pl
from jax.experimental.pallas import tpu as pltpu
from jax.sharding import Mesh, PartitionSpec as P

inv_temp = 10.0
epsilon = 1e-06
tile = 256
group = ("yh", "yl", "core")
sizes = {"z": 8, "x": 4, "yh": 4, "yl": 2, "core": 2}
mib = 1024 * 1024


def halves(array):
    high = array.astype(jnp.bfloat16)
    low = (array - high.astype(jnp.float32)).astype(jnp.bfloat16)
    return high, low


def as_column(row):
    return jnp.transpose(jnp.broadcast_to(row, (128, row.shape[1])))[:, 0:1]


def as_row(column):
    return jnp.transpose(jnp.broadcast_to(column, (column.shape[0], 128)))[0:1, :]


def column_ids(first, count):
    place = lax.broadcasted_iota(jnp.int32, (1, count), 1)
    return first + (place >> 6) * 1024 + (place & 63)


def score_kernel(firsts, rows, cols, partner, exps, sums, col_high, col_low):
    step = pl.program_id(0)

    @pl.when(step == 0)
    def _():
        high, low = halves(cols[...])
        col_high[...] = high
        col_low[...] = low

    row_high, row_low = halves(rows[...] * inv_temp)
    nt = functools.partial(
        lax.dot_general,
        dimension_numbers=(((1,), (1,)), ((), ())),
        preferred_element_type=jnp.float32,
    )
    scores = (
        nt(row_high, col_high[...]) + nt(row_high, col_low[...]) + nt(row_low, col_high[...])
    )
    ids = column_ids(firsts[1], cols.shape[0])
    row_ids = firsts[0] + step * tile + lax.broadcasted_iota(jnp.int32, (tile, 1), 0)
    exp_scores = jnp.where(row_ids == ids, 0.0, jnp.exp(scores))
    exps[...] = exp_scores
    hits = jnp.where(as_column(partner[...]) == ids, scores, 0.0)
    sums[0:1, :] = as_row(jnp.sum(exp_scores, axis=1, keepdims=True))
    sums[1:2, :] = as_row(jnp.sum(hits, axis=1, keepdims=True))


def grad_kernel(firsts, exps, cols, partner, own, seen, out, col_high, col_low):
    step = pl.program_id(0)

    @pl.when(step == 0)
    def _():
        high, low = halves(cols[...])
        col_high[...] = high
        col_low[...] = low

    ids = column_ids(firsts[1], cols.shape[0])
    paired = as_column(partner[...]) == ids
    own_scale, own_weight = as_column(own[0:1, :]), as_column(own[1:2, :])
    weights = exps[...] * (own_scale + seen[0:1, :]) - jnp.where(
        paired, own_weight + seen[1:2, :], 0.0
    )
    high, low = halves(weights)
    nn = functools.partial(jnp.dot, preferred_element_type=jnp.float32)
    sums = nn(high, col_high[...]) + nn(high, col_low[...]) + nn(low, col_high[...])
    for part in range(4):
        out[part % 2, 0, part // 2] = sums[part * 64 : (part + 1) * 64]


def scores_of(firsts, rows, cols, partner):
    count, width = rows.shape
    seen = cols.shape[0]
    return pl.pallas_call(
        score_kernel,
        grid=(count // tile,),
        in_specs=[
            pl.BlockSpec(memory_space=pltpu.SMEM),
            pl.BlockSpec((tile, width), lambda i: (i, 0)),
            pl.BlockSpec((seen, width), lambda i: (0, 0)),
            pl.BlockSpec((1, tile), lambda i: (0, i)),
        ],
        out_specs=[
            pl.BlockSpec((tile, seen), lambda i: (i, 0)),
            pl.BlockSpec((2, tile), lambda i: (0, i)),
        ],
        out_shape=[
            jax.ShapeDtypeStruct((count, seen), jnp.float32),
            jax.ShapeDtypeStruct((2, count), jnp.float32),
        ],
        scratch_shapes=[pltpu.VMEM((seen, width), jnp.bfloat16)] * 2,
        compiler_params=pltpu.CompilerParams(vmem_limit_bytes=40 * mib),
        cost_estimate=pl.CostEstimate(
            flops=6 * count * seen * width,
            bytes_accessed=4 * (count * seen + (count + seen) * width),
            transcendentals=count * seen,
        ),
    )(firsts, rows, cols, partner)


def grads_of(firsts, exps, cols, partner, own, seen):
    count, seen_count = exps.shape
    width = cols.shape[1]
    return pl.pallas_call(
        grad_kernel,
        grid=(count // tile,),
        in_specs=[
            pl.BlockSpec(memory_space=pltpu.SMEM),
            pl.BlockSpec((tile, seen_count), lambda i: (i, 0)),
            pl.BlockSpec((seen_count, width), lambda i: (0, 0)),
            pl.BlockSpec((1, tile), lambda i: (0, i)),
            pl.BlockSpec((2, tile), lambda i: (0, i)),
            pl.BlockSpec((2, seen_count), lambda i: (0, 0)),
        ],
        out_specs=pl.BlockSpec((2, 1, 2, 64, width), lambda i: (0, i, 0, 0, 0)),
        out_shape=jax.ShapeDtypeStruct((2, count // tile, 2, 64, width), jnp.float32),
        scratch_shapes=[pltpu.VMEM((seen_count, width), jnp.bfloat16)] * 2,
        compiler_params=pltpu.CompilerParams(vmem_limit_bytes=40 * mib),
        cost_estimate=pl.CostEstimate(
            flops=6 * count * seen_count * width,
            bytes_accessed=4 * (count * seen_count + (count + seen_count) * width),
            transcendentals=0,
        ),
    )(firsts, exps, cols, partner, own, seen)


def told_all(part, axes, count):
    return lax.all_to_all(jnp.broadcast_to(part[None], (count,) + part.shape), axes, 0, 0, tiled=True)


def per_device(projections, partner, cotangent):
    at = {name: lax.axis_index(name) for name in sizes}
    member = at["yl"] * 2 + at["core"]
    row_norms = jnp.sqrt(jnp.sum(projections * projections, axis=1, keepdims=True) + epsilon)
    unit = projections / row_norms
    quarter = lax.dynamic_slice_in_dim(unit, member * 64, 64, 0)
    cols = lax.all_gather(lax.all_gather(quarter, "x", tiled=True), "z", tiled=True)
    rows = lax.all_gather(unit, "yh", tiled=True)
    partner_rows = lax.all_gather(partner, "yh", tiled=True)
    weight_rows = lax.all_gather(cotangent, "yh", tiled=True)
    firsts = jnp.stack([(at["z"] * 4 + at["x"]) * 1024, at["yh"] * 256 + member * 64])
    exps, part_sums = scores_of(firsts, rows, cols, partner_rows[None])
    sums = jnp.sum(told_all(part_sums, group, 16), axis=0)
    losses = jnp.log(sums[0]) - sums[1]
    row_loss = lax.dynamic_slice_in_dim(losses, at["yh"] * 256, 256, 0)
    own = jnp.stack([weight_rows / sums[0], weight_rows])
    own_part = lax.dynamic_slice_in_dim(own, at["yh"] * 256 + member * 64, 64, 1)
    seen = jnp.swapaxes(told_all(own_part, ("z", "x"), 32), 0, 1).reshape(2, -1)
    partial = grads_of(firsts, exps, cols, partner_rows[None], own, seen)
    halved = jnp.sum(lax.all_to_all(partial, "core", 0, 0, tiled=True), axis=0)
    swapped = lax.all_to_all(halved.reshape(8, 64, 256), ("yh", "yl"), 0, 0, tiled=True)
    grad_quarter = inv_temp * jnp.sum(swapped, axis=0)
    norm_quarter = lax.dynamic_slice_in_dim(row_norms, member * 64, 64, 0)
    along = jnp.sum(quarter * grad_quarter, axis=1, keepdims=True)
    grad_quarter = (grad_quarter - quarter * along) / norm_quarter
    return row_loss, lax.all_gather(grad_quarter, ("yl", "core"), tiled=True)


def solution(mesh):
    fine = Mesh(mesh.devices.reshape(tuple(sizes.values())), tuple(sizes))
    blocks = ("z", "x", "yh")
    return jax.shard_map(
        per_device,
        mesh=fine,
        in_specs=(P(blocks, None), P(blocks), P(blocks)),
        out_specs=(P(blocks), P(blocks, None)),
        check_vma=False,
    )
```

time: 2050 us -> 202 us (0.10)
  waiting for transfers between devices: 1310 us -> 86.9 us
  starting transfers between devices: 512 us -> 22.8 us
  matrix products: 109 us -> 0 us
  blocking collectives: 77.9 us -> 46 us
    ppermute x258 -> x0, waiting for transfers between devices: 1240 us -> none  [passed_along(): lax.ppermute(array, axis, [(i, (i + by) % length) for i in range(length)])]
    ppermute x258 -> x0, starting transfers between devices: 512 us -> none  [passed_along(): lax.ppermute(array, axis, [(i, (i + by) % length) for i in range(length)])]
    dot_general x260 -> x0, matrix products: 109 us -> none  [the longest x130 57.6 us: scores_of(): lax.dot_general(seen_rows, unit_rows, (((1,), (1,)), ((), ())), precision...]
    psum x1 -> x0, blocking collectives: 77.9 us -> none  [combine(): return lax.psum(payload, 'rep')]
    psum x1 -> x0, waiting for transfers between devices: 64.4 us -> none  [combine(): return lax.psum(payload, 'rep')]
    all_gather x0 -> x2, waiting for transfers between devices: none -> 61 us  [the longest x1 40.6 us: per_device(): lax.all_gather(lax.all_gather(quarter, 'x', tiled=True), 'z', tiled=True)]
    all_gather x0 -> x4, blocking collectives: none -> 38.3 us  [the longest x1 11.3 us: per_device(): lax.all_gather(quarter, 'x', tiled=True)]
    all_to_all x0 -> x3, waiting for transfers between devices: none -> 25.8 us  [the longest x1 17.2 us: per_device(): lax.all_to_all(halved.reshape(8, 64, 256), ('yh', 'yl'), 0, 0, tiled=True)]
  transfers between devices with their start and end apart: 259 -> 5, of which waited for: 131 -> 4; matrix products, arithmetic and copies ran while one was open for 6% -> 1% of each run, Pallas kernels for 0% -> 0%
where the time goes in v1:
time: 202 us
  waiting for transfers between devices  86.9 us (43%)
  blocking collectives  46 us (23%)
  starting transfers between devices  22.8 us (11%)
  between operations  14.2 us (7%)
  local copies, waits for them, and re-layouts  13.8 us (7%)
  Pallas kernels  13 us (6%)
  other arithmetic  4.9 us (2%)
    all_gather x1, waiting for transfers between devices, per_device(): lax.all_gather(lax.all_gather(quarter, 'x', tiled=True), 'z', tiled=True)  40.6 us
    all_gather x1, waiting for transfers between devices, per_device(): rows = lax.all_gather(unit, 'yh', tiled=True)  20.4 us
    all_to_all x2, starting transfers between devices, told_all(): lax.all_to_all(jnp.broadcast_to(part[None], (count,) + part.shape), axes,...  18.2 us
    all_to_all x1, waiting for transfers between devices, per_device(): lax.all_to_all(halved.reshape(8, 64, 256), ('yh', 'yl'), 0, 0, tiled=True)  17.2 us
    all_gather x1, blocking collectives, per_device(): lax.all_gather(quarter, 'x', tiled=True)  11.3 us
    unnamed x17, local copies, waits for them, and re-layouts  10.9 us
    all_gather x1, blocking collectives, per_device(): partner_rows = lax.all_gather(partner, 'yh', tiled=True)  10.9 us
    all_gather x1, blocking collectives, per_device(): weight_rows = lax.all_gather(cotangent, 'yh', tiled=True)  10 us
  transfers between devices with their start and end apart: 5, of which 4 were waited for; matrix products, arithmetic and copies ran while one was open for 1% of the time, Pallas kernels for 0%

profile of v1, /device:TPU:1, one launch (start us, length us, event | category | flops | bytes accessed | tf_op | source)
XLA Modules:
  0.0 201.5 jit_solution(2474562135808617514)
XLA Ops:
  7.2 0.0 copy-start.6
  7.2 0.0 all-gather.5.cloned.1.call-start
  7.2 1.1 multiply_reduce_fusion
  8.3 1.8 broadcast_divide_fusion
  10.1 0.0 all-gather.5.cloned.1.call-update
  10.1 0.0 all-gather.7.cloned.1.call-start
  10.1 0.8 constant_dynamic-slice_fusion
  11.0 11.3 %all_gather.19 = f32[256,256]{1,0:T(8,128)} all-gather(f32[64,256]{1,0:T(8,128)S(1)} %constant_dynamic-slice_fusion), channel_id=1, replica_groups=mesh['z'=8,'x'=4,'yh'=4,'yl'=2,'core'=2] {'x'}, dimensions={0}, use_global_device_ids=true | all-gather | bytes 327680 | tf_op jit(solution)/shard_map/all_gather | solution.py:152
  22.3 0.0 all-gather.7.cloned.1.call-update
  22.3 10.9 %all-gather = s32[4,1,256]{2,1,0:T(1,128)S(1)} all-gather(s32[1,1,256]{2,1,0:T(1,128)} %bitcast.22), channel_id=1, replica_groups=mesh['z'=8,'x'=4,'yh'=4,'yl'=2,'core'=2] {'yh'}, dimensions={0}, use_global_device_ids=true | all-gather | bytes 5120 | tf_op jit(solution)/shard_map/all_gather | solution.py:154
  33.2 0.1 pad_add_fusion.firsts
  33.3 20.4 %all-gather.5.cloned.1.call-done.rows = f32[1024,256]{1,0:T(8,128)} async-done(((f32[256,256]{1,0:T(8,128)}), f32[1024,256]{1,0:T(8,128)}) %all-gather.5.cloned.1.call-update) | async-done | bytes 1048592 | tf_op jit(solution)/shard_map/all_gather | solution.py:153
  53.7 40.6 %all-gather.7.cloned.1.call-done.cols = f32[2048,256]{1,0:T(8,128)} async-done(((f32[256,256]{1,0:T(8,128)}), f32[2048,256]{1,0:T(8,128)}) %all-gather.7.cloned.1.call-update) | async-done | bytes 2097168 | tf_op jit(solution)/shard_map/all_gather | solution.py:152
  94.3 0.0 copy-start
  94.3 1.6 copy-done
  95.9 0.0 copy-start.2
  95.9 1.2 copy-done.2
  97.1 0.0 copy-start.1
  97.1 6.7 %shard_map.50 = (f32[1024,2048]{1,0:T(8,128)S(1)}, f32[2,1024]{1,0:T(2,128)S(1)}) custom-call(s32[2]{0:T(128)S(1)} %pad_add_fusion.firsts, f32[1024,256]{1,0:T(8,128)S(1)} %copy-done.2, f32[2048,256]{1,0:T(8,128)S(1)} %copy-done, s32[1,1024]{1,0:T(1,128)S(1)} %bitcast.12), custom_call_target="tpu_custom_call" | custom-call | flops 3221225472 | bytes 11534336 | tf_op jit(solution)/shard_map/pallas_call | solution.py:89
  103.8 0.0 copy-start.3
  103.8 3.2 %copy-done.3 = f32[1024,2048]{1,0:T(8,128)} copy-done((f32[1024,2048]{1,0:T(8,128)}, f32[1024,2048]{1,0:T(8,128)S(1)}, u32[]{:S(2)}) %copy-start.3) | copy-done | bytes 8388632
  107.0 0.7 broadcast_in_dim.7
  107.7 11.5 %all-to-all-start = ((f32[16,2,1024]{2,1,0:T(2,128)}), f32[16,2,1024]{2,1,0:T(2,128)S(1)}, u32[]{:S(2)}, u32[]{:S(2)}) async-start(f32[16,2,1024]{2,1,0:T(2,128)} %broadcast_in_dim.7), calls=%async_computation | async-start | bytes 262144 | tf_op jit(solution)/shard_map/all_to_all | solution.py:143
  119.2 0.0 copy-done.6
  119.2 10.0 %all-gather.1 = f32[4,1,256]{2,1,0:T(1,128)S(1)} all-gather(f32[1,1,256]{2,1,0:T(1,128)S(1)} %bitcast.23), channel_id=1, replica_groups=mesh['z'=8,'x'=4,'yh'=4,'yl'=2,'core'=2] {'yh'}, dimensions={0}, use_global_device_ids=true | all-gather | bytes 5120 | tf_op jit(solution)/shard_map/all_gather | solution.py:155
  129.2 0.0 all-to-all-done
  129.2 0.1 reduce_sum.46
  129.3 0.1 fusion
  129.4 0.7 reshape.38
  130.1 6.7 %all-to-all-start.1 = ((f32[32,1,128]{2,1,0:T(1,128)}), f32[32,1,128]{2,1,0:T(1,128)S(1)}, u32[]{:S(2)}, u32[]{:S(2)}) async-start(f32[32,1,128]{2,1,0:T(1,128)} %reshape.38), calls=%async_computation.1 | async-start | bytes 32768 | tf_op jit(solution)/shard_map/all_to_all | solution.py:143
  136.8 8.6 %all-to-all-done.1 = f32[32,1,128]{2,1,0:T(1,128)S(1)} async-done(((f32[32,1,128]{2,1,0:T(1,128)}), f32[32,1,128]{2,1,0:T(1,128)S(1)}, u32[]{:S(2)}, u32[]{:S(2)}) %all-to-all-start.1) | async-done | bytes 16416 | tf_op jit(solution)/shard_map/all_to_all | solution.py:143
  145.4 0.5 broadcast.15
  145.9 0.7 reduce
  146.6 0.1 reshape.39
  146.7 0.1 reshape.30.seen
  146.8 0.0 copy-done.1
  146.8 0.0 copy-start.4
  146.8 3.4 %copy-done.4 = f32[1024,2048]{1,0:T(8,128)S(1)} copy-done((f32[1024,2048]{1,0:T(8,128)S(1)}, f32[1024,2048]{1,0:T(8,128)}, u32[]{:S(2)}) %copy-start.4) | copy-done | bytes 8388632
  150.1 0.0 copy-start.5
  150.1 6.3 %shard_map.51 = f32[2,4,2,64,256]{4,3,2,1,0:T(8,128)S(1)} custom-call(s32[2]{0:T(128)S(1)} %pad_add_fusion.firsts, f32[1024,2048]{1,0:T(8,128)S(1)} %copy-done.4, f32[2048,256]{1,0:T(8,128)S(1)} %copy-done.1, s32[1,1024]{1,0:T(1,128)S(1)} %bitcast.13, f32[2,1024]{1,0:T(2,128)S(1)} %pad_maximum_fusion.own, f32[2,2048]{1,0:T(2,128)S(1)} %reshape.30.seen), custom_call_target="tpu_custom_call" | custom-call | flops 3221225472 | bytes 11534336 | tf_op jit(solution)/shard_map/pallas_call | solution.py:119
  156.4 7.7 %all_to_all.20 = f32[2,4,2,64,256]{4,3,2,1,0:T(8,128)S(1)} all-to-all(f32[2,4,2,64,256]{4,3,2,1,0:T(8,128)S(1)} %shard_map.51), channel_id=1, replica_groups=mesh['z'=8,'x'=4,'yh'=4,'yl'=2,'core'=2] {'core'}, dimensions={0} | all-to-all | bytes 2097152 | tf_op jit(solution)/shard_map/all_to_all | solution.py:165
  164.1 0.9 reduce_sum.47
  165.0 4.6 %all-to-all-start.3 = ((f32[8,64,256]{2,1,0:T(8,128)}), f32[8,64,256]{2,1,0:T(8,128)S(1)}, u32[]{:S(2)}, u32[]{:S(2)}) async-start(f32[8,64,256]{2,1,0:T(8,128)} %bitcast.11), calls=%async_computation.3 | async-start | bytes 1048576 | tf_op jit(solution)/shard_map/all_to_all | solution.py:166
  169.6 0.1 dynamic-slice.3
  169.7 0.6 dynamic_slice.11
  170.3 17.2 %all-to-all-done.3 = f32[8,64,256]{2,1,0:T(8,128)S(1)} async-done(((f32[8,64,256]{2,1,0:T(8,128)}), f32[8,64,256]{2,1,0:T(8,128)S(1)}, u32[]{:S(2)}, u32[]{:S(2)}) %all-to-all-start.3) | async-done | bytes 524320 | tf_op jit(solution)/shard_map/all_to_all | solution.py:166
  187.6 0.0 copy-done.5
  187.6 0.1 multiply_reduce_fusion.1
  187.7 0.1 subtract_divide_fusion
  187.9 6.1 %all_gather.23 = f32[256,256]{1,0:T(8,128)S(1)} all-gather(f32[64,256]{1,0:T(8,128)S(1)} %subtract_divide_fusion), channel_id=1, replica_groups=mesh['z'=8,'x'=4,'yh'=4,'yl'=2,'core'=2] {'yl','core'}, dimensions={0}, use_global_device_ids=true | all-gather | bytes 327680 | tf_op jit(solution)/shard_map/all_gather | solution.py:171
  194.0 0.7 copy.13
  (7 shorter events, 0.1 us)
Async XLA Ops:
  7.2 112.0 %copy-start.6 = (f32[256]{0:T(256)S(1)}, f32[256]{0:T(256)}, u32[]{:S(2)}) copy-start(f32[256]{0:T(256)} %param.5) | copy-start | bytes 3076
  7.2 46.5 %all-gather.5.cloned.1.call-start = ((), (), s32[]{:S(2)}) async-start(), calls=%async_computation.4 | async-start | bytes 1310720 | tf_op jit(solution)/shard_map/all_gather | solution.py:153
  10.1 84.2 %all-gather.7.cloned.1.call-start = ((), (), s32[]{:S(2)}) async-start(), calls=%async_computation.5 | async-start | bytes 2359296 | tf_op jit(solution)/shard_map/all_gather | solution.py:152
  94.3 1.6 copy-start
  95.9 1.2 copy-start.2
  97.1 49.7 %copy-start.1 = (f32[2048,256]{1,0:T(8,128)S(1)}, f32[2048,256]{1,0:T(8,128)}, u32[]{:S(2)}) copy-start(f32[2048,256]{1,0:T(8,128)} %all-gather.7.cloned.1.call-done.cols) | copy-start | bytes 6291460
  103.8 3.2 %copy-start.3 = (f32[1024,2048]{1,0:T(8,128)}, f32[1024,2048]{1,0:T(8,128)S(1)}, u32[]{:S(2)}) copy-start(f32[1024,2048]{1,0:T(8,128)S(1)} %get-tuple-element.5.exps) | copy-start | bytes 25165828
  107.7 21.5 %all-to-all-start = ((f32[16,2,1024]{2,1,0:T(2,128)}), f32[16,2,1024]{2,1,0:T(2,128)S(1)}, u32[]{:S(2)}, u32[]{:S(2)}) async-start(f32[16,2,1024]{2,1,0:T(2,128)} %broadcast_in_dim.7), calls=%async_computation | async-start | bytes 262144 | tf_op jit(solution)/shard_map/all_to_all | solution.py:143
  130.1 15.3 %all-to-all-start.1 = ((f32[32,1,128]{2,1,0:T(1,128)}), f32[32,1,128]{2,1,0:T(1,128)S(1)}, u32[]{:S(2)}, u32[]{:S(2)}) async-start(f32[32,1,128]{2,1,0:T(1,128)} %reshape.38), calls=%async_computation.1 | async-start | bytes 32768 | tf_op jit(solution)/shard_map/all_to_all | solution.py:143
  146.8 3.4 %copy-start.4 = (f32[1024,2048]{1,0:T(8,128)S(1)}, f32[1024,2048]{1,0:T(8,128)}, u32[]{:S(2)}) copy-start(f32[1024,2048]{1,0:T(8,128)} %copy-done.3) | copy-start | bytes 25165828
  150.1 37.5 %copy-start.5 = (f32[256,256]{1,0:T(8,128)S(1)}, f32[256,256]{1,0:T(8,128)}, u32[]{:S(2)}) copy-start(f32[256,256]{1,0:T(8,128)} %broadcast_divide_fusion) | copy-start | bytes 786436
  165.0 22.6 %all-to-all-start.3 = ((f32[8,64,256]{2,1,0:T(8,128)}), f32[8,64,256]{2,1,0:T(8,128)S(1)}, u32[]{:S(2)}, u32[]{:S(2)}) async-start(f32[8,64,256]{2,1,0:T(8,128)} %bitcast.11), calls=%async_computation.3 | async-start | bytes 1048576 | tf_op jit(solution)/shard_map/all_to_all | solution.py:166
Sparse Core Ops, SparseCore 0:
  10.7 42.9 all-gather.4
  55.8 38.4 all-gather.6

commit v2 on v1

v2 whole, which is shorter than its diff:
```python
import math

import jax
import jax.numpy as jnp
from jax import lax
from jax.experimental import pallas as pl
from jax.experimental.pallas import tpu as pltpu
from jax.sharding import Mesh, PartitionSpec as P

inv_temp = 10.0
epsilon = 1e-06
tile = 256
lanes = 128
quarter = 64
packed = 264
group = ("yh", "yl", "core")
sizes = {"z": 8, "x": 4, "yh": 4, "yl": 2, "core": 2}
steps = (0, 3, 1, 2)
mib = 1024 * 1024
f32, bf16 = jnp.float32, jnp.bfloat16


def halves(array):
    high = array.astype(bf16)
    low = (array - high.astype(f32)).astype(bf16)
    return high, low


def as_column(row):
    return jnp.transpose(jnp.broadcast_to(row, (lanes, row.shape[1])))


def dot(left, right, dims=((1,), (0,))):
    return lax.dot_general(left, right, (dims, ((), ())), preferred_element_type=f32)


def products(left, right, dims=((1,), (0,))):
    return dot(left[0], right[0], dims) + dot(left[0], right[1], dims) + dot(left[1], right[0], dims)


def pieces(array):
    return [array[:, at : at + lanes] for at in range(0, array.shape[1], lanes)]


def fetch(sems, *pairs):
    copies = [pltpu.make_async_copy(a, b, sems.at[i]) for i, (a, b) in enumerate(pairs)]
    for copy in copies:
        copy.start()
    return copies


def wait_all(copies):
    for copy in copies:
        copy.wait()


def blocks_of(ref):
    return [ref.at[pl.ds(at, tile), :] for at in range(0, ref.shape[0], tile)]


def info_pairs(rows, info):
    return [(rows.at[block, pl.ds(tile, 8), :], info.at[block]) for block in range(rows.shape[0])]


def member():
    return lax.axis_index("yl") * 2 + lax.axis_index("core")


def source_of(chunk):
    return lax.rem(lax.axis_index("x") + steps[chunk], 4)


def seen_ids(chunk, count):
    first = source_of(chunk) * 1024 + lax.axis_index("yh") * 256 + member() * quarter
    place = lax.broadcasted_iota(jnp.int32, (1, count), 1)
    return first + (place >> 6) * 4096 + (place & 63)


def start_kernel(
    rows, partner, cotangent, packed_rows, told, unit, norms, partner_in, cotangent_in, packed_in,
    sems,
):
    copies = fetch(
        sems,
        (rows, packed_in.at[pl.ds(0, tile), :]),
        (partner, partner_in),
        (cotangent, cotangent_in),
    )
    packed_in[tile:, :] = jnp.zeros((packed - tile, rows.shape[1]), f32)
    wait_all(copies)
    packed_in[tile : tile + 1, :] = partner_in[...].astype(f32)
    packed_in[tile + 1 : tile + 2, :] = cotangent_in[...]
    copies = fetch(sems, (packed_in, packed_rows))
    own = packed_in[pl.ds(pl.multiple_of(member() * quarter, quarter), quarter), :]
    own_norms = jnp.sqrt(jnp.sum(own * own, axis=1, keepdims=True) + epsilon)
    own_unit = own / own_norms
    unit[...] = own_unit
    norms[...] = jnp.broadcast_to(own_norms, norms.shape)
    told[...] = jnp.broadcast_to(own_unit[None], told.shape)
    wait_all(copies)


def rows_kernel(rows, high, low, partner):
    for block in range(rows.shape[0]):
        at = slice(block * tile, (block + 1) * tile)
        raw = rows[block, :tile, :]
        norms = jnp.sqrt(jnp.sum(raw * raw, axis=1, keepdims=True) + epsilon)
        high[at, :], low[at, :] = halves(raw / norms * (inv_temp * math.log2(math.e)))
        partner[at, :] = as_column(rows[block, tile : tile + 1, :]).astype(jnp.int32)


def score(chunk, at, row_high, row_low, cols, partner, count):
    scores = products((row_high[at, :], row_low[at, :]), cols, ((1,), (1,)))
    ids = seen_ids(chunk, count)
    exps = jnp.exp2(scores)
    if chunk == 0:
        first = (lax.axis_index("z") * 4 + lax.axis_index("x")) * 1024 + at.start
        row_ids = first + lax.broadcasted_iota(jnp.int32, (tile, 1), 0)
        exps = jnp.where(row_ids == ids, 0.0, exps)
    paired = [partner[at, :] == piece for piece in pieces(ids)]
    hits = [jnp.where(p, s, 0.0) for p, s in zip(paired, pieces(scores))]
    return exps, paired, jnp.sum(exps, axis=0, keepdims=True), sum(hits[1:], hits[0])


def paired_sum_of(paired, cols):
    ones = jnp.concatenate([p.astype(f32).astype(bf16) for p in paired], axis=1)
    return dot(ones, cols[0]) + dot(ones, cols[1])


def chunk_kernel(chunk, row_high, row_low, cols, partner, *refs):
    before, refs = refs[: 3 if chunk else 0], refs[3 if chunk else 0 :]
    high_out, low_out, col_sums, hits, plain, paired_rows, high, low, sems = refs
    count = cols.shape[0]
    parts = halves(cols[...])
    copies, totals = [], None
    for block in range(row_high.shape[0] // tile):
        at = slice(block * tile, (block + 1) * tile)
        exps, paired, total, hit = score(chunk, at, row_high, row_low, parts, partner, count)
        totals = total if totals is None else totals + total
        high[at, :], low[at, :] = exp_parts = halves(exps)
        rows_at = pl.ds(at.start, tile)
        copies += fetch(
            sems.at[block],
            (high.at[rows_at, :], high_out.at[rows_at, :]),
            (low.at[rows_at, :], low_out.at[rows_at, :]),
        )
        sums = (hit, products(exp_parts, parts), paired_sum_of(paired, parts))
        for i, (ref, value) in enumerate(zip((hits, plain, paired_rows), sums)):
            ref[at, :] = value + before[i][at, :] if chunk else value
    for part, piece in enumerate(pieces(totals)):
        col_sums[part : part + 1, :] = piece
    wait_all(copies)


def last_kernel(
    row_high, row_low, cols, partner, hits, plain, cotangent, sums_0, sums_1, sums_2, high_out,
    low_out, told, shared, high, low, sums, sems,
):
    count = cols.shape[0]
    parts = halves(cols[...])
    copies, totals = [], None
    for block in range(row_high.shape[0] // tile):
        at = slice(block * tile, (block + 1) * tile)
        exps, _, total, hit = score(3, at, row_high, row_low, parts, partner, count)
        totals = total if totals is None else totals + total
        high[at, :], low[at, :] = exp_parts = halves(exps)
        rows_at = pl.ds(at.start, tile)
        copies += fetch(
            sems.at[block],
            (high.at[rows_at, :], high_out.at[rows_at, :]),
            (low.at[rows_at, :], low_out.at[rows_at, :]),
        )
        summed = products(exp_parts, parts) + plain[at, :]
        hit += hits[at, :]
        for part in range(tile // lanes):
            turned = jnp.transpose(hit[part * lanes : (part + 1) * lanes, :])
            row = math.log(2.0) * jnp.sum(turned, axis=0, keepdims=True)
            for side in range(2):
                k = block * 4 + part * 2 + side
                shared[k, :quarter, :] = summed[(part * 2 + side) * 64 : (part * 2 + side + 1) * 64]
                shared[k, quarter:, :] = jnp.zeros((8, shared.shape[2]), f32)
                here = row if side == 0 else pltpu.roll(row, 64, 1)
                shared[k, quarter : quarter + 1, :lanes] = here
    own = cotangent[pl.ds(lax.axis_index("yl"), 1), :]
    own = jnp.where(lax.axis_index("core") == 0, own, pltpu.roll(own, 64, 1))
    last = jnp.concatenate(pieces(totals), axis=0)
    for chunk, values in enumerate((sums_0[...], sums_1[...], sums_2[...], last)):
        for part in range(4):
            sums[pl.ds(source_of(chunk) * 4 + part, 1), :] = values[part : part + 1, :]
    sums[16:17, :] = own
    sums[17:, :] = jnp.zeros((7, lanes), f32)
    told[...] = jnp.broadcast_to(sums[...][None], told.shape)
    wait_all(copies)


def shadow_kernel(cols, rows, before, out, cols_in, info, paired_rows, sems):
    copies = fetch(sems, (cols, cols_in), (before, paired_rows), *info_pairs(rows, info))
    wait_all(copies)
    parts = halves(cols_in[...])
    ids = pieces(seen_ids(3, cols_in.shape[0]))
    for block in range(paired_rows.shape[0] // tile):
        at = slice(block * tile, (block + 1) * tile)
        partner = as_column(info[block, 0:1, :]).astype(jnp.int32)
        paired_rows[at, :] += paired_sum_of([partner == piece for piece in ids], parts)
    wait_all(fetch(sems, (paired_rows, out)))


def grad_kernel(message, *refs):
    ins, (out, own_sum, *refs) = refs[:14], refs[14:]
    exps, cols, (paired_rows, rows) = ins[:8], ins[8:12], ins[12:]
    exps_in, refs = refs[:8], refs[8:]
    cols_in, paired_in, info, scales, weights, au_high, au_low, total, sems = refs
    arrivals = []
    for chunk in range(4):
        pairs = [(ref, exps_in[i]) for i, ref in enumerate(exps) if i % 4 == chunk]
        arrivals.append(fetch(sems.at[chunk], (cols[chunk], cols_in.at[chunk]), *pairs))
    last = fetch(sems.at[4], (paired_rows, paired_in), *info_pairs(rows, info))
    scales[...] = jnp.sum(message[...], axis=0)[:16, :]
    sums = []
    place = lax.broadcasted_iota(jnp.int32, (1, lanes), 1)
    for chunk in range(4):
        source = source_of(chunk)
        for z in range(0, 8, 2):
            even, odd = (message[(z + side) * 4 + source, 16:17, :] for side in range(2))
            row = chunk * 4 + z // 2
            sums.append(scales[pl.ds(source * 4 + z // 2, 1), :])
            weights[row : row + 1, :] = jnp.where(place < 64, even, pltpu.roll(odd, 64, 1))
    z = lax.axis_index("z")
    own = scales[pl.ds(lax.axis_index("x") * 4 + z // 2, 1), :]
    own_sum[...] = jnp.where(lax.rem(z, 2) == 0, own, pltpu.roll(own, 64, 1))
    columns = jnp.transpose(jnp.concatenate([weights[...] / jnp.concatenate(sums, axis=0)] * 8, axis=0))
    count = cols_in.shape[1]
    ids = []
    for chunk, arrival in enumerate(arrivals):
        arrival[0].wait()
        for part in range(4):
            scaled = cols_in[chunk, part * lanes : (part + 1) * lanes, :]
            scaled *= columns[:, chunk * 4 + part : chunk * 4 + part + 1]
            at = slice(chunk * count + part * lanes, chunk * count + (part + 1) * lanes)
            au_high[at, :], au_low[at, :] = halves(scaled)
        at = slice(chunk * count, (chunk + 1) * count)
        scaled_cols = (au_high[at, :], au_low[at, :])
        ids += pieces(seen_ids(chunk, count))
        wait_all(arrival[1:])
        for block in range(4):
            rows_at = slice(block * tile, (block + 1) * tile)
            added = products(
                (exps_in[chunk][rows_at, :], exps_in[4 + chunk][rows_at, :]), scaled_cols
            )
            total[rows_at, :] = added if chunk == 0 else total[rows_at, :] + added
    wait_all(last)
    for block in range(4):
        rows_at = slice(block * tile, (block + 1) * tile)
        partner = as_column(info[block, 0:1, :]).astype(jnp.int32)
        spread = jnp.zeros((tile, lanes), f32)
        for i, piece in enumerate(ids):
            spread += jnp.where(partner == piece, weights[i : i + 1, :], 0.0)
        weight = as_column(info[block, 1:2, :])[:, :1] + jnp.sum(spread, axis=1, keepdims=True)
        result = total[rows_at, :] - weight * paired_in[rows_at, :]
        for part in range(4):
            out[part % 2, block, part // 2] = result[part * 64 : (part + 1) * 64]


def final_kernel(parts, shared, own_sum, cotangent, unit, norms, out):
    own = cotangent[pl.ds(lax.axis_index("yl"), 1), :]
    own = jnp.where(lax.axis_index("core") == 0, own, pltpu.roll(own, 64, 1))
    scale = as_column(own / own_sum[...])[:quarter, :1]
    grad = inv_temp * (jnp.sum(parts[...], axis=0) + scale * shared[:quarter, :])
    along = jnp.sum(unit[...] * grad, axis=1, keepdims=True)
    out[:quarter, :] = (grad - unit[...] * along) / norms[:, :1]
    out[quarter:, :] = jnp.zeros((8, out.shape[1]), f32)
    out[quarter : quarter + 1, :lanes] = jnp.log(own_sum[...]) - shared[quarter : quarter + 1, :lanes]


vmem, anywhere = pl.BlockSpec(memory_space=pltpu.VMEM), pl.BlockSpec(memory_space=pl.ANY)


def call(kernel, outs, args, limit, cost=None, scratch=(), far=(), far_outs=()):
    args = [
        pltpu.with_memory_space_constraint(arg, pltpu.HBM) if i in far else arg
        for i, arg in enumerate(args)
    ]
    return pl.pallas_call(
        kernel,
        in_specs=[anywhere if i in far else vmem for i in range(len(args))],
        out_specs=[anywhere if i in far_outs else vmem for i in range(len(outs))],
        out_shape=[
            pltpu.HBM(*out) if i in far_outs else jax.ShapeDtypeStruct(*out)
            for i, out in enumerate(outs)
        ],
        scratch_shapes=list(scratch),
        compiler_params=pltpu.CompilerParams(vmem_limit_bytes=limit * mib),
        cost_estimate=cost,
    )(*args)


def estimate(passes, count, seen, width, exps=0):
    return pl.CostEstimate(
        flops=passes * 2 * count * seen * width,
        bytes_accessed=4 * (count * seen + (count + seen) * width),
        transcendentals=exps,
    )


def passed_along(array, by):
    return lax.ppermute(array, "x", [(i, (i + by) % 4) for i in range(4)])


def per_device(projections, partner, cotangent):
    width = projections.shape[1]
    count, seen = 4 * tile, 8 * quarter
    copies = pltpu.SemaphoreType.DMA
    info = pltpu.VMEM((4, 8, width), f32)
    packed_rows, told, own_unit, norms = call(
        start_kernel,
        [((packed, width), f32), ((8, quarter, width), f32), ((quarter, width), f32),
         ((quarter, lanes), f32)],
        (projections, partner[None], cotangent[None]),
        4,
        scratch=[pltpu.VMEM((1, tile), jnp.int32), pltpu.VMEM((1, tile), f32),
                 pltpu.VMEM((packed, width), f32), copies((3,))],
        far=(0, 1, 2),
        far_outs=(0,),
    )
    here = lax.all_to_all(told, "z", 0, 0, tiled=True).reshape(seen, width)
    rows = lax.all_gather(packed_rows, "yh")
    cols = [here, passed_along(here, 1), passed_along(here, -1), passed_along(here, 2)]
    row_high, row_low, partners = call(
        rows_kernel,
        [((count, width), bf16)] * 2 + [((count, lanes), jnp.int32)],
        (rows,),
        8,
    )
    exps_out = [((count, seen), bf16)] * 2
    row_sums = [((count, width), f32)] * 2
    own_exps = [pltpu.VMEM(*out) for out in exps_out]
    own_rows = [pltpu.VMEM(*out) for out in row_sums]
    highs, lows, col_sums, before = [], [], [], ()
    for chunk in range(3):

        def kernel(*refs, chunk=chunk):
            chunk_kernel(chunk, *refs)

        high, low, sums, *before = call(
            kernel,
            exps_out + [((seen // lanes, lanes), f32), ((count, lanes), f32)] + row_sums,
            (row_high, row_low, cols[chunk], partners, *before),
            24,
            estimate(8, count, seen, width, count * seen),
            own_exps + [copies((4, 2))],
            far_outs=(0, 1),
        )
        highs.append(high)
        lows.append(low)
        col_sums.append(sums)
    hits, plain, paired_rows = before
    high, low, told, shared = call(
        last_kernel,
        exps_out + [((32, 24, lanes), f32), ((16, quarter + 8, width), f32)],
        (row_high, row_low, cols[3], partners, hits, plain, cotangent.reshape(2, lanes), *col_sums),
        24,
        estimate(6, count, seen, width, count * seen),
        own_exps + [pltpu.VMEM((24, lanes), f32), copies((4, 2))],
        far_outs=(0, 1),
    )
    highs.append(high)
    lows.append(low)
    shared = lax.psum_scatter(shared.reshape(-1, width), group, tiled=True)
    message = lax.all_to_all(told, ("z", "x"), 0, 0, tiled=True)
    (paired_rows,) = call(
        shadow_kernel,
        row_sums[:1],
        (cols[3], rows, paired_rows),
        16,
        estimate(2, count, seen, width),
        [pltpu.VMEM((seen, width), f32), info, own_rows[0], copies((6,))],
        far=range(3),
        far_outs=(0,),
    )
    partial, own_sum = call(
        grad_kernel,
        [((2, 4, 2, quarter, width), f32), ((1, lanes), f32)],
        (message, *highs, *lows, *cols, paired_rows, rows),
        28,
        estimate(3, count, 4 * seen, width),
        own_exps * 4
        + [pltpu.VMEM((4, seen, width), f32), own_rows[0], info]
        + [pltpu.VMEM((16, lanes), f32)] * 2
        + [pltpu.VMEM((4 * seen, width), bf16)] * 2
        + [own_rows[0], copies((5, 5))],
        far=range(1, 15),
    )
    halved = jnp.sum(lax.all_to_all(partial, "core", 0, 0, tiled=True), axis=0)
    swapped = lax.all_to_all(halved.reshape(8, quarter, width), ("yh", "yl"), 0, 0, tiled=True)
    (result,) = call(
        final_kernel,
        [((quarter + 8, width), f32)],
        (swapped, shared, own_sum, cotangent.reshape(2, lanes), own_unit, norms),
        4,
    )
    result = lax.all_gather(result, ("yl", "core"))
    return result[:, quarter, :quarter].reshape(-1), result[:, :quarter].reshape(-1, width)


def solution(mesh):
    fine = Mesh(mesh.devices.reshape(tuple(sizes.values())), tuple(sizes))
    blocks = ("z", "x", "yh")
    return jax.shard_map(
        per_device,
        mesh=fine,
        in_specs=(P(blocks, None), P(blocks), P(blocks)),
        out_specs=(P(blocks), P(blocks, None)),
        check_vma=False,
    )
```

time: 202 us -> 151 us (0.75)
  waiting for transfers between devices: 86.9 us -> 21.6 us
  blocking collectives: 46 us -> 62 us
  Pallas kernels: 13 us -> 28.4 us
  local copies, waits for them, and re-layouts: 13.8 us -> 3.53 us
  other arithmetic: 4.9 us -> 0.12 us
  starting transfers between devices: 22.8 us -> 19.6 us
    all_gather x2 -> x1, waiting for transfers between devices: 61 us -> 8.11 us  [per_device(): rows = lax.all_gather(packed_rows, 'yh')]
    all_to_all x0 -> x2, blocking collectives: none -> 46.7 us  [the longest x1 26.7 us: per_device(): here = lax.all_to_all(told, 'z', 0, 0, tiled=True).reshape(seen, width)]
    all_gather x4 -> x1, blocking collectives: 38.3 us -> 8.3 us  [per_device(): result = lax.all_gather(result, ('yl', 'core'))]
    all_to_all x3 -> x1, waiting for transfers between devices: 25.8 us -> 10.3 us  [per_device(): message = lax.all_to_all(told, ('z', 'x'), 0, 0, tiled=True)]
    pallas_call x2 -> x9, Pallas kernels: 13 us -> 28.4 us  [call(): pl.pallas_call(kernel, in_specs=[anywhere if i in far else vmem for i in...]
    all_to_all x3 -> x1, starting transfers between devices: 22.8 us -> 9.6 us  [per_device(): message = lax.all_to_all(told, ('z', 'x'), 0, 0, tiled=True)]
    ppermute x0 -> x3, starting transfers between devices: none -> 9.92 us  [passed_along(): return lax.ppermute(array, 'x', [(i, (i + by) % 4) for i in range(4)])]
    unnamed x17 -> x16, local copies, waits for them, and re-layouts: 10.9 us -> 2.15 us
  transfers between devices with their start and end apart: 5 -> 6, of which waited for: 4 -> 3; matrix products, arithmetic and copies ran while one was open for 1% -> 0% of each run, Pallas kernels for 0% -> 15%
where the time goes in v2:
time: 151 us; the launch traced here: 150 us
  blocking collectives  62 us (41%)
  Pallas kernels  28.4 us (19%)
  waiting for transfers between devices  21.6 us (14%)
  starting transfers between devices  19.6 us (13%)
  between operations  14.3 us (9%)
  local copies, waits for them, and re-layouts  3.53 us (2%)
    pallas_call x9, Pallas kernels, call(): pl.pallas_call(kernel, in_specs=[anywhere if i in far else vmem for i in...  28.4 us
    all_to_all x1, blocking collectives, per_device(): here = lax.all_to_all(told, 'z', 0, 0, tiled=True).reshape(seen, width)  26.7 us
    all_to_all x1, blocking collectives, per_device(): lax.all_to_all(halved.reshape(8, quarter, width), ('yh', 'yl'), 0, 0, til...  20.1 us
    all_to_all x1, waiting for transfers between devices, per_device(): message = lax.all_to_all(told, ('z', 'x'), 0, 0, tiled=True)  10.3 us
    ppermute x3, starting transfers between devices, passed_along(): return lax.ppermute(array, 'x', [(i, (i + by) % 4) for i in range(4)])  9.92 us
    all_to_all x1, starting transfers between devices, per_device(): message = lax.all_to_all(told, ('z', 'x'), 0, 0, tiled=True)  9.6 us
    all_gather x1, blocking collectives, per_device(): result = lax.all_gather(result, ('yl', 'core'))  8.3 us
    all_gather x1, waiting for transfers between devices, per_device(): rows = lax.all_gather(packed_rows, 'yh')  8.11 us
  transfers between devices with their start and end apart: 6, of which 3 were waited for; matrix products, arithmetic and copies ran while one was open for 0% of the time, Pallas kernels for 15%

profile of v2, /device:TPU:1, one launch (start us, length us, event | category | flops | bytes accessed | tf_op | source)
XLA Modules:
  0.0 149.5 jit_solution(1178183056057941049)
XLA Ops:
  7.2 0.0 all-gather.4.cloned.1.call-start
  7.2 1.7 %shard_map.50 = (f32[264,256]{1,0:T(8,128)}, f32[8,64,256]{2,1,0:T(8,128)S(1)}, f32[64,256]{1,0:T(8,128)S(1)}, f32[64,128]{1,0:T(8,128)S(1)}) custom-call(f32[256,256]{1,0:T(8,128)} %rows.1, s32[1,256]{1,0:T(1,128)} %bitcast.24, f32[1,256]{1,0:T(1,128)} %bitcast.17), custom_call_target="tpu_custom_call" | custom-call | tf_op jit(solution)/shard_map/pallas_call | solution.py:283
  8.9 0.0 all-gather.4.cloned.1.call-update
  8.9 0.0 reduce-scatter.2.cloned.1.call-start
  9.0 26.7 %all_to_all.20 = f32[8,64,256]{2,1,0:T(8,128)S(1)} all-to-all(f32[8,64,256]{2,1,0:T(8,128)S(1)} %get-tuple-element.36), channel_id=1, replica_groups=mesh['z'=8,'x'=4,'yh'=4,'yl'=2,'core'=2] {'z'}, dimensions={0} | all-to-all | bytes 1048576 | tf_op jit(solution)/shard_map/all_to_all | solution.py:325
  35.6 0.0 copy-start.2
  35.6 3.1 %collective-permute-start.2 = (f32[512,256]{1,0:T(8,128)S(1)}, f32[512,256]{1,0:T(8,128)S(1)}, u32[]{:S(2)}, u32[]{:S(2)}) collective-permute-start(f32[512,256]{1,0:T(8,128)S(1)} %bitcast.12), channel_id=1, source_target_pairs={{0,16},{16,32},{32,48},{48,0},{1,17},{17,33},{33,49},{49,1},{2,18}... | collective-permute-start | bytes 1572872 | tf_op jit(solution)/shard_map/ppermute | solution.py:306
  38.7 3.4 %collective-permute-start.1 = (f32[512,256]{1,0:T(8,128)S(1)}, f32[512,256]{1,0:T(8,128)S(1)}, u32[]{:S(2)}, u32[]{:S(2)}) collective-permute-start(f32[512,256]{1,0:T(8,128)S(1)} %bitcast.13), channel_id=1, source_target_pairs={{0,48},{16,0},{32,16},{48,32},{1,49},{17,1},{33,17},{49,33},{2,50}... | collective-permute-start | bytes 1572872 | tf_op jit(solution)/shard_map/ppermute | solution.py:306
  42.1 3.4 %collective-permute-start = (f32[512,256]{1,0:T(8,128)S(1)}, f32[512,256]{1,0:T(8,128)S(1)}, u32[]{:S(2)}, u32[]{:S(2)}) collective-permute-start(f32[512,256]{1,0:T(8,128)S(1)} %bitcast.14), channel_id=1, source_target_pairs={{0,32},{16,48},{32,0},{48,16},{1,33},{17,49},{33,1},{49,17},{2,34}... | collective-permute-start | bytes 1572872 | tf_op jit(solution)/shard_map/ppermute | solution.py:306
  45.6 8.1 %all-gather.4.cloned.1.call-done = f32[1056,256]{1,0:T(8,128)} async-done(((f32[264,256]{1,0:T(8,128)}), f32[1056,256]{1,0:T(8,128)}) %all-gather.4.cloned.1.call-update) | async-done | bytes 1081360 | tf_op jit(solution)/shard_map/all_gather | solution.py:326
  53.7 0.0 copy-start
  53.7 1.2 copy-done
  54.9 0.5 shard_map.51
  55.5 4.0 %shard_map.52 = (bf16[1024,512]{1,0:T(8,128)(2,1)}, bf16[1024,512]{1,0:T(8,128)(2,1)}, f32[4,128]{1,0:T(4,128)S(1)}, f32[1024,128]{1,0:T(8,128)S(1)}, f32[1024,256]{1,0:T(8,128)S(1)}, /*index=5*/f32[1024,256]{1,0:T(8,128)S(1)}) custom-call(bf16[1024,256]{1,0:T(8,128)(2,1)S(1)} %get-tuple-element.34.refs_0_.row_high, ...), custom_call_target="tpu_custom_call" | custom-call | flops 2147483648 | bytes 3670016 | tf_op jit(solution)/shard_map/pallas_call | solution.py:283
  59.5 0.0 copy-done.2
  59.5 0.0 collective-permute-done.2.refs_2_.refs_9_
  59.5 0.0 copy-start.4
  59.5 3.8 %shard_map.53 = (bf16[1024,512]{1,0:T(8,128)(2,1)}, bf16[1024,512]{1,0:T(8,128)(2,1)}, f32[4,128]{1,0:T(4,128)S(1)}, f32[1024,128]{1,0:T(8,128)S(1)}, f32[1024,256]{1,0:T(8,128)S(1)}, /*index=5*/f32[1024,256]{1,0:T(8,128)S(1)}) custom-call(bf16[1024,256]{1,0:T(8,128)(2,1)S(1)} %get-tuple-element.34.refs_0_.row_high, ...), custom_call_target="tpu_custom_call" | custom-call | flops 2147483648 | bytes 3670016 | tf_op jit(solution)/shard_map/pallas_call | solution.py:283
  63.3 0.0 copy-done.4
  63.3 0.0 collective-permute-done.1.refs_2_.refs_10_
  63.3 0.0 copy-start.5
  63.3 0.0 copy-start.7
  63.3 3.8 %shard_map.54 = (bf16[1024,512]{1,0:T(8,128)(2,1)}, bf16[1024,512]{1,0:T(8,128)(2,1)}, f32[4,128]{1,0:T(4,128)S(1)}, f32[1024,128]{1,0:T(8,128)S(1)}, f32[1024,256]{1,0:T(8,128)S(1)}, /*index=5*/f32[1024,256]{1,0:T(8,128)S(1)}) custom-call(bf16[1024,256]{1,0:T(8,128)(2,1)S(1)} %get-tuple-element.34.refs_0_.row_high, ...), custom_call_target="tpu_custom_call" | custom-call | flops 2147483648 | bytes 3670016 | tf_op jit(solution)/shard_map/pallas_call | solution.py:283
  67.2 0.0 copy-done.5
  67.2 0.0 copy-start.3
  67.2 0.0 collective-permute-done.cols.refs_11_
  67.2 0.0 copy-start.1
  67.2 0.0 copy-done.7
  67.2 4.0 %shard_map.55 = (bf16[1024,512]{1,0:T(8,128)(2,1)}, bf16[1024,512]{1,0:T(8,128)(2,1)}, f32[32,24,128]{2,1,0:T(8,128)}, f32[16,72,256]{2,1,0:T(8,128)}) custom-call(bf16[1024,256]{1,0:T(8,128)(2,1)S(1)} %get-tuple-element.34.refs_0_.row_high, bf16[1024,256]{1,0:T(8,128)(2,1)S(1)} %get-tuple-element.35.refs_1_.row_low, ...), custom_call_target="tpu_custom_call" | custom-call | flops 1610612736 | bytes 3670016 | tf_op jit(solution)/shard_map/pallas_call | solution.py:283
  71.2 0.0 copy-done.3
  71.2 0.0 copy-done.1
  71.2 0.0 reduce-scatter.2.cloned.1.call-update
  71.2 9.6 %all-to-all-start.1 = ((f32[32,24,128]{2,1,0:T(8,128)}), f32[32,24,128]{2,1,0:T(8,128)S(1)}, u32[]{:S(2)}, u32[]{:S(2)}) async-start(f32[32,24,128]{2,1,0:T(8,128)} %get-tuple-element.49), calls=%async_computation.1 | async-start | bytes 786432 | tf_op jit(solution)/shard_map/all_to_all | solution.py:369
  80.8 3.2 %shard_map.56.refs_12_ = f32[1024,256]{1,0:T(8,128)} custom-call(f32[512,256]{1,0:T(8,128)} %copy-done.1, f32[4,264,256]{2,1,0:T(8,128)} %bitcast.9, f32[1024,256]{1,0:T(8,128)} %copy-done.3), custom_call_target="tpu_custom_call" | custom-call | flops 536870912 | bytes 3670016 | tf_op jit(solution)/shard_map/pallas_call | solution.py:283
  84.0 10.3 %all-to-all-done.1.message = f32[32,24,128]{2,1,0:T(8,128)S(1)} async-done(((f32[32,24,128]{2,1,0:T(8,128)}), f32[32,24,128]{2,1,0:T(8,128)S(1)}, u32[]{:S(2)}, u32[]{:S(2)}) %all-to-all-start.1) | async-done | bytes 393248 | tf_op jit(solution)/shard_map/all_to_all | solution.py:369
  94.3 7.1 %shard_map.57 = (f32[2,4,2,64,256]{4,3,2,1,0:T(8,128)S(1)}, f32[1,128]{1,0:T(1,128)S(1)}) custom-call(f32[32,24,128]{2,1,0:T(8,128)S(1)} %all-to-all-done.1.message, bf16[1024,512]{1,0:T(8,128)(2,1)} %get-tuple-element.50.refs_0_, bf16[1024,512]{1,0:T(8,128)(2,1)} %get-tuple-element.51.refs_1_, bf16[1024,512]{1,0:T(8,128)(2,1)} %get-tuple-element.52.refs_2_, ...), custom_call_target="tpu_custom_call" | custom-call | flops 3221225472 | bytes 11534336 | tf_op jit(solution)/shard_map/pallas_call | solution.py:283
  101.5 7.0 %all_to_all.21 = f32[2,4,2,64,256]{4,3,2,1,0:T(8,128)S(1)} all-to-all(f32[2,4,2,64,256]{4,3,2,1,0:T(8,128)S(1)} %get-tuple-element.59), channel_id=1, replica_groups=mesh['z'=8,'x'=4,'yh'=4,'yl'=2,'core'=2] {'core'}, dimensions={0} | all-to-all | bytes 2097152 | tf_op jit(solution)/shard_map/all_to_all | solution.py:393
  108.5 0.1 reduce_sum.9
  108.6 20.1 %all_to_all.22.parts = f32[8,64,256]{2,1,0:T(8,128)S(1)} all-to-all(f32[8,64,256]{2,1,0:T(8,128)S(1)} %bitcast.20), channel_id=1, replica_groups=mesh['z'=8,'x'=4,'yh'=4,'yl'=2,'core'=2] {'yh','yl'}, dimensions={0} | all-to-all | bytes 1048576 | tf_op jit(solution)/shard_map/all_to_all | solution.py:394
  128.7 3.1 %reduce-scatter.2.cloned.1.call-done.shared = f32[72,256]{1,0:T(8,128)} async-done(((f32[1152,256]{1,0:T(8,128)}), f32[72,256]{1,0:T(8,128)}) %reduce-scatter.2.cloned.1.call-update) | async-done | bytes 73744 | tf_op jit(solution)/shard_map/reduce_scatter | solution.py:368
  131.8 0.0 copy-start.6
  131.8 0.9 copy-done.6
  132.7 0.3 shard_map.58
  133.0 8.3 %all-gather.1 = f32[288,256]{1,0:T(8,128)S(1)} all-gather(f32[72,256]{1,0:T(8,128)S(1)} %shard_map.58), channel_id=3, replica_groups=mesh['z'=8,'x'=4,'yh'=4,'yl'=2,'core'=2] {'yl','core'}, dimensions={0}, use_global_device_ids=true | all-gather | bytes 368640 | tf_op jit(solution)/shard_map/all_gather | solution.py:401
  141.3 0.7 slice.9
  142.1 0.6 reshape_squeeze.3
  (1 shorter events, 0.0 us)
Async XLA Ops:
  7.2 46.5 %all-gather.4.cloned.1.call-start = ((), (), s32[]{:S(2)}) async-start(), calls=%async_computation.6 | async-start | bytes 1351680 | tf_op jit(solution)/shard_map/all_gather | solution.py:326
  8.9 122.9 %reduce-scatter.2.cloned.1.call-start = ((), (), s32[]{:S(2)}) async-start(), calls=%async_computation.5 | async-start | bytes 1253376 | tf_op jit(solution)/shard_map/reduce_scatter | solution.py:368
  35.6 23.9 %copy-start.2 = (f32[8,64,256]{2,1,0:T(8,128)}, f32[8,64,256]{2,1,0:T(8,128)S(1)}, u32[]{:S(2)}) copy-start(f32[8,64,256]{2,1,0:T(8,128)S(1)} %all_to_all.20) | copy-start | bytes 1572868
  35.6 23.9 %collective-permute-start.2 = (f32[512,256]{1,0:T(8,128)S(1)}, f32[512,256]{1,0:T(8,128)S(1)}, u32[]{:S(2)}, u32[]{:S(2)}) collective-permute-start(f32[512,256]{1,0:T(8,128)S(1)} %bitcast.12), channel_id=1, source_target_pairs={{0,16},{16,32},{32,48},{48,0},{1,17},{17,33},{33,49},{49,1},{2,18}... | collective-permute-start | bytes 1572872 | tf_op jit(solution)/shard_map/ppermute | solution.py:306
  38.7 24.6 %collective-permute-start.1 = (f32[512,256]{1,0:T(8,128)S(1)}, f32[512,256]{1,0:T(8,128)S(1)}, u32[]{:S(2)}, u32[]{:S(2)}) collective-permute-start(f32[512,256]{1,0:T(8,128)S(1)} %bitcast.13), channel_id=1, source_target_pairs={{0,48},{16,0},{32,16},{48,32},{1,49},{17,1},{33,17},{49,33},{2,50}... | collective-permute-start | bytes 1572872 | tf_op jit(solution)/shard_map/ppermute | solution.py:306
  42.1 25.1 %collective-permute-start = (f32[512,256]{1,0:T(8,128)S(1)}, f32[512,256]{1,0:T(8,128)S(1)}, u32[]{:S(2)}, u32[]{:S(2)}) collective-permute-start(f32[512,256]{1,0:T(8,128)S(1)} %bitcast.14), channel_id=1, source_target_pairs={{0,32},{16,48},{32,0},{48,16},{1,33},{17,49},{33,1},{49,17},{2,34}... | collective-permute-start | bytes 1572872 | tf_op jit(solution)/shard_map/ppermute | solution.py:306
  53.7 1.2 copy-start
  59.5 3.8 %copy-start.4 = (f32[512,256]{1,0:T(8,128)}, f32[512,256]{1,0:T(8,128)S(1)}, u32[]{:S(2)}) copy-start(f32[512,256]{1,0:T(8,128)S(1)} %collective-permute-done.2.refs_2_.refs_9_) | copy-start | bytes 1572868
  63.3 3.9 %copy-start.5 = (f32[512,256]{1,0:T(8,128)}, f32[512,256]{1,0:T(8,128)S(1)}, u32[]{:S(2)}) copy-start(f32[512,256]{1,0:T(8,128)S(1)} %collective-permute-done.1.refs_2_.refs_10_) | copy-start | bytes 1572868
  63.3 3.9 %copy-start.7 = (f32[256]{0:T(256)S(1)}, f32[256]{0:T(256)}, u32[]{:S(2)}) copy-start(f32[256]{0:T(256)} %param.5) | copy-start | bytes 3076
  67.2 4.0 %copy-start.3 = (f32[1024,256]{1,0:T(8,128)}, f32[1024,256]{1,0:T(8,128)S(1)}, u32[]{:S(2)}) copy-start(f32[1024,256]{1,0:T(8,128)S(1)} %get-tuple-element.58.before) | copy-start | bytes 3145732
  67.2 4.0 %copy-start.1 = (f32[512,256]{1,0:T(8,128)}, f32[512,256]{1,0:T(8,128)S(1)}, u32[]{:S(2)}) copy-start(f32[512,256]{1,0:T(8,128)S(1)} %collective-permute-done.cols.refs_11_) | copy-start | bytes 1572868
  71.2 23.1 %all-to-all-start.1 = ((f32[32,24,128]{2,1,0:T(8,128)}), f32[32,24,128]{2,1,0:T(8,128)S(1)}, u32[]{:S(2)}, u32[]{:S(2)}) async-start(f32[32,24,128]{2,1,0:T(8,128)} %get-tuple-element.49), calls=%async_computation.1 | async-start | bytes 786432 | tf_op jit(solution)/shard_map/all_to_all | solution.py:369
  131.8 0.9 copy-start.6
Sparse Core Ops, SparseCore 0:
  10.1 43.5 all-gather.3
  71.4 60.4 reduce-scatter.1

commit v3 on v2

--- a/solution.py
+++ b/solution.py
@@ -117,35 +117,33 @@
         first = (lax.axis_index("z") * 4 + lax.axis_index("x")) * 1024 + at.start
         row_ids = first + lax.broadcasted_iota(jnp.int32, (tile, 1), 0)
         exps = jnp.where(row_ids == ids, 0.0, exps)
-    paired = [partner[at, :] == piece for piece in pieces(ids)]
-    hits = [jnp.where(p, s, 0.0) for p, s in zip(paired, pieces(scores))]
-    return exps, paired, jnp.sum(exps, axis=0, keepdims=True), sum(hits[1:], hits[0])
-
-
-def paired_sum_of(paired, cols):
-    ones = jnp.concatenate([p.astype(f32).astype(bf16) for p in paired], axis=1)
-    return dot(ones, cols[0]) + dot(ones, cols[1])
+    hits = [
+        jnp.where(partner[at, :] == piece, part, 0.0)
+        for piece, part in zip(pieces(ids), pieces(scores))
+    ]
+    return exps, jnp.sum(exps, axis=0, keepdims=True), sum(hits[1:], hits[0])
+
+
+def send_parts(sems, at, parts, held, outs):
+    rows_at = pl.ds(at.start, tile)
+    for ref, part in zip(held, parts):
+        ref[at, :] = part
+    return fetch(sems, *[(a.at[rows_at, :], b.at[rows_at, :]) for a, b in zip(held, outs)])
 
 
 def chunk_kernel(chunk, row_high, row_low, cols, partner, *refs):
-    before, refs = refs[: 3 if chunk else 0], refs[3 if chunk else 0 :]
-    high_out, low_out, col_sums, hits, plain, paired_rows, high, low, sems = refs
+    before, refs = refs[: 2 if chunk else 0], refs[2 if chunk else 0 :]
+    high_out, low_out, col_sums, hits, plain, high, low, sems = refs
     count = cols.shape[0]
     parts = halves(cols[...])
     copies, totals = [], None
     for block in range(row_high.shape[0] // tile):
         at = slice(block * tile, (block + 1) * tile)
-        exps, paired, total, hit = score(chunk, at, row_high, row_low, parts, partner, count)
+        exps, total, hit = score(chunk, at, row_high, row_low, parts, partner, count)
         totals = total if totals is None else totals + total
-        high[at, :], low[at, :] = exp_parts = halves(exps)
-        rows_at = pl.ds(at.start, tile)
-        copies += fetch(
-            sems.at[block],
-            (high.at[rows_at, :], high_out.at[rows_at, :]),
-            (low.at[rows_at, :], low_out.at[rows_at, :]),
-        )
-        sums = (hit, products(exp_parts, parts), paired_sum_of(paired, parts))
-        for i, (ref, value) in enumerate(zip((hits, plain, paired_rows), sums)):
+        exp_parts = halves(exps)
+        copies += send_parts(sems.at[block], at, exp_parts, (high, low), (high_out, low_out))
+        for i, (ref, value) in enumerate(zip((hits, plain), (hit, products(exp_parts, parts)))):
             ref[at, :] = value + before[i][at, :] if chunk else value
     for part, piece in enumerate(pieces(totals)):
         col_sums[part : part + 1, :] = piece
@@ -153,25 +151,25 @@
 
 
 def last_kernel(
-    row_high, row_low, cols, partner, hits, plain, cotangent, sums_0, sums_1, sums_2, high_out,
-    low_out, told, shared, high, low, sums, sems,
+    row_high, row_low, cols_2, cols_3, partner, hits, plain, cotangent, sums_0, sums_1, high_2,
+    low_2, high_3, low_3, told, shared, *refs,
 ):
-    count = cols.shape[0]
-    parts = halves(cols[...])
-    copies, totals = [], None
+    *held, sums, sems = refs
+    count = cols_2.shape[0]
+    outs = (high_2, low_2, high_3, low_3)
+    parts = [halves(cols_2[...]), halves(cols_3[...])]
+    copies, totals = [], [None, None]
     for block in range(row_high.shape[0] // tile):
         at = slice(block * tile, (block + 1) * tile)
-        exps, _, total, hit = score(3, at, row_high, row_low, parts, partner, count)
-        totals = total if totals is None else totals + total
-        high[at, :], low[at, :] = exp_parts = halves(exps)
-        rows_at = pl.ds(at.start, tile)
-        copies += fetch(
-            sems.at[block],
-            (high.at[rows_at, :], high_out.at[rows_at, :]),
-            (low.at[rows_at, :], low_out.at[rows_at, :]),
-        )
-        summed = products(exp_parts, parts) + plain[at, :]
-        hit += hits[at, :]
+        summed, hit = plain[at, :], hits[at, :]
+        for i in range(2):
+            exps, total, more = score(2 + i, at, row_high, row_low, parts[i], partner, count)
+            totals[i] = total if block == 0 else totals[i] + total
+            exp_parts = halves(exps)
+            ends = slice(2 * i, 2 * i + 2)
+            copies += send_parts(sems.at[block * 2 + i], at, exp_parts, held[ends], outs[ends])
+            summed += products(exp_parts, parts[i])
+            hit += more
         for part in range(tile // lanes):
             turned = jnp.transpose(hit[part * lanes : (part + 1) * lanes, :])
             row = math.log(2.0) * jnp.sum(turned, axis=0, keepdims=True)
@@ -183,8 +181,8 @@
                 shared[k, quarter : quarter + 1, :lanes] = here
     own = cotangent[pl.ds(lax.axis_index("yl"), 1), :]
     own = jnp.where(lax.axis_index("core") == 0, own, pltpu.roll(own, 64, 1))
-    last = jnp.concatenate(pieces(totals), axis=0)
-    for chunk, values in enumerate((sums_0[...], sums_1[...], sums_2[...], last)):
+    late = [jnp.concatenate(pieces(total), axis=0) for total in totals]
+    for chunk, values in enumerate((sums_0[...], sums_1[...], *late)):
         for part in range(4):
             sums[pl.ds(source_of(chunk) * 4 + part, 1), :] = values[part : part + 1, :]
     sums[16:17, :] = own
@@ -193,15 +191,22 @@
     wait_all(copies)
 
 
-def shadow_kernel(cols, rows, before, out, cols_in, info, paired_rows, sems):
-    copies = fetch(sems, (cols, cols_in), (before, paired_rows), *info_pairs(rows, info))
+def shadow_kernel(cols_0, cols_1, cols_2, cols_3, rows, out, cols_in, info, paired_rows, sems):
+    cols = (cols_0, cols_1, cols_2, cols_3)
+    copies = fetch(
+        sems, *[(ref, cols_in.at[i]) for i, ref in enumerate(cols)], *info_pairs(rows, info)
+    )
     wait_all(copies)
-    parts = halves(cols_in[...])
-    ids = pieces(seen_ids(3, cols_in.shape[0]))
-    for block in range(paired_rows.shape[0] // tile):
-        at = slice(block * tile, (block + 1) * tile)
-        partner = as_column(info[block, 0:1, :]).astype(jnp.int32)
-        paired_rows[at, :] += paired_sum_of([partner == piece for piece in ids], parts)
+    partners = [as_column(info[i, 0:1, :]).astype(jnp.int32) for i in range(4)]
+    for chunk in range(4):
+        parts = halves(cols_in[chunk])
+        ids = pieces(seen_ids(chunk, cols_in.shape[1]))
+        for block, partner in enumerate(partners):
+            at = slice(block * tile, (block + 1) * tile)
+            ones = [(partner == piece).astype(f32).astype(bf16) for piece in ids]
+            ones = jnp.concatenate(ones, axis=1)
+            added = dot(ones, parts[0]) + dot(ones, parts[1])
+            paired_rows[at, :] = paired_rows[at, :] + added if chunk else added
     wait_all(fetch(sems, (paired_rows, out)))
 
 
@@ -261,7 +266,9 @@
             out[part % 2, block, part // 2] = result[part * 64 : (part + 1) * 64]
 
 
-def final_kernel(parts, shared, own_sum, cotangent, unit, norms, out):
+def final_kernel(parts, here, there, own_sum, cotangent, unit, norms, out):
+    mine = pl.ds(pl.multiple_of(lax.axis_index("core") * (quarter + 8), 8), quarter + 8)
+    shared = here[mine, :] + there[mine, :]
     own = cotangent[pl.ds(lax.axis_index("yl"), 1), :]
     own = jnp.where(lax.axis_index("core") == 0, own, pltpu.roll(own, 64, 1))
     scale = as_column(own / own_sum[...])[:quarter, :1]
@@ -336,45 +343,46 @@
     own_exps = [pltpu.VMEM(*out) for out in exps_out]
     own_rows = [pltpu.VMEM(*out) for out in row_sums]
     highs, lows, col_sums, before = [], [], [], ()
-    for chunk in range(3):
+    for chunk in range(2):
 
         def kernel(*refs, chunk=chunk):
             chunk_kernel(chunk, *refs)
 
         high, low, sums, *before = call(
             kernel,
-            exps_out + [((seen // lanes, lanes), f32), ((count, lanes), f32)] + row_sums,
+            exps_out + [((seen // lanes, lanes), f32), ((count, lanes), f32)] + row_sums[:1],
             (row_high, row_low, cols[chunk], partners, *before),
             24,
-            estimate(8, count, seen, width, count * seen),
+            estimate(6, count, seen, width, count * seen),
             own_exps + [copies((4, 2))],
             far_outs=(0, 1),
         )
         highs.append(high)
         lows.append(low)
         col_sums.append(sums)
-    hits, plain, paired_rows = before
-    high, low, told, shared = call(
+    hits, plain = before
+    high_2, low_2, high_3, low_3, told, shared = call(
         last_kernel,
-        exps_out + [((32, 24, lanes), f32), ((16, quarter + 8, width), f32)],
-        (row_high, row_low, cols[3], partners, hits, plain, cotangent.reshape(2, lanes), *col_sums),
-        24,
-        estimate(6, count, seen, width, count * seen),
-        own_exps + [pltpu.VMEM((24, lanes), f32), copies((4, 2))],
-        far_outs=(0, 1),
-    )
-    highs.append(high)
-    lows.append(low)
-    shared = lax.psum_scatter(shared.reshape(-1, width), group, tiled=True)
+        exps_out * 2 + [((32, 24, lanes), f32), ((16, quarter + 8, width), f32)],
+        (row_high, row_low, *cols[2:], partners, hits, plain, cotangent.reshape(2, lanes), *col_sums),
+        32,
+        estimate(6, count, 2 * seen, width, 2 * count * seen),
+        own_exps * 2 + [pltpu.VMEM((24, lanes), f32), copies((8, 2))],
+        far_outs=range(4),
+    )
+    highs += [high_2, high_3]
+    lows += [low_2, low_3]
+    here = lax.psum_scatter(shared.reshape(-1, width), ("yh", "yl"), tiled=True)
+    there = lax.ppermute(here, "core", [(0, 1), (1, 0)])
     message = lax.all_to_all(told, ("z", "x"), 0, 0, tiled=True)
     (paired_rows,) = call(
         shadow_kernel,
         row_sums[:1],
-        (cols[3], rows, paired_rows),
-        16,
-        estimate(2, count, seen, width),
-        [pltpu.VMEM((seen, width), f32), info, own_rows[0], copies((6,))],
-        far=range(3),
+        (*cols, rows),
+        24,
+        estimate(2, count, 4 * seen, width),
+        [pltpu.VMEM((4, seen, width), f32), info, own_rows[0], copies((8,))],
+        far=range(5),
         far_outs=(0,),
     )
     partial, own_sum = call(
@@ -395,7 +403,7 @@
     (result,) = call(
         final_kernel,
         [((quarter + 8, width), f32)],
-        (swapped, shared, own_sum, cotangent.reshape(2, lanes), own_unit, norms),
+        (swapped, here, there, own_sum, cotangent.reshape(2, lanes), own_unit, norms),
         4,
     )
     result = lax.all_gather(result, ("yl", "core"))

time: 151 us -> 145 us (0.960)
  blocking collectives: 62 us -> 39.8 us
  waiting for transfers between devices: 21.6 us -> 32.6 us
  starting transfers between devices: 19.6 us -> 27 us
  Pallas kernels: 28.4 us -> 26.6 us
    all_to_all x1 -> x0, blocking collectives: 20.1 us -> none  [per_device(): lax.all_to_all(halved.reshape(8, quarter, width), ('yh', 'yl'), 0, 0, til...]
    all_to_all x0 -> x1, waiting for transfers between devices: none -> 15.4 us  [per_device(): lax.all_to_all(halved.reshape(8, quarter, width), ('yh', 'yl'), 0, 0, til...]
    all_to_all x0 -> x1, starting transfers between devices: none -> 5.34 us  [per_device(): lax.all_to_all(halved.reshape(8, quarter, width), ('yh', 'yl'), 0, 0, til...]
    reduce_scatter x1, waiting for transfers between devices: 3.14 us -> 0.01 us  [per_device(): here = lax.psum_scatter(shared.reshape(-1, width), ('yh', 'yl'), tiled=True)]
    ppermute x0 -> x1, starting transfers between devices: none -> 2.56 us  [per_device(): there = lax.ppermute(here, 'core', [(0, 1), (1, 0)])]
    all_gather x1, blocking collectives: 8.3 us -> 6.2 us  [per_device(): result = lax.all_gather(result, ('yl', 'core'))]
    pallas_call x9 -> x8, Pallas kernels: 28.4 us -> 26.6 us  [call(): pl.pallas_call(kernel, in_specs=[anywhere if i in far else vmem for i in...]
    all_to_all x1, waiting for transfers between devices: 10.3 us -> 8.54 us  [per_device(): message = lax.all_to_all(told, ('z', 'x'), 0, 0, tiled=True)]
  transfers between devices with their start and end apart: 6 -> 8, of which waited for: 3 -> 4; matrix products, arithmetic and copies ran while one was open for 0% -> 1% of each run, Pallas kernels for 15% -> 13%
where the time goes in v3:
time: 145 us
  blocking collectives  39.8 us (27%)
  waiting for transfers between devices  32.6 us (22%)
  starting transfers between devices  27 us (19%)
  Pallas kernels  26.6 us (18%)
  between operations  14.2 us (10%)
  local copies, waits for them, and re-layouts  3.56 us (2%)
    all_to_all x1, blocking collectives, per_device(): here = lax.all_to_all(told, 'z', 0, 0, tiled=True).reshape(seen, width)  26.7 us
    pallas_call x8, Pallas kernels, call(): pl.pallas_call(kernel, in_specs=[anywhere if i in far else vmem for i in...  26.6 us
    all_to_all x1, waiting for transfers between devices, per_device(): lax.all_to_all(halved.reshape(8, quarter, width), ('yh', 'yl'), 0, 0, til...  15.4 us
    ppermute x3, starting transfers between devices, passed_along(): return lax.ppermute(array, 'x', [(i, (i + by) % 4) for i in range(4)])  9.92 us
    all_to_all x1, starting transfers between devices, per_device(): message = lax.all_to_all(told, ('z', 'x'), 0, 0, tiled=True)  9.14 us
    all_to_all x1, waiting for transfers between devices, per_device(): message = lax.all_to_all(told, ('z', 'x'), 0, 0, tiled=True)  8.54 us
    all_gather x1, waiting for transfers between devices, per_device(): rows = lax.all_gather(packed_rows, 'yh')  8.1 us
    all_to_all x1, blocking collectives, per_device(): halved = jnp.sum(lax.all_to_all(partial, 'core', 0, 0, tiled=True), axis=0)  6.96 us
  transfers between devices with their start and end apart: 8, of which 4 were waited for; matrix products, arithmetic and copies ran while one was open for 1% of the time, Pallas kernels for 13%

profile of v3, /device:TPU:1, one launch (start us, length us, event | category | flops | bytes accessed | tf_op | source)
XLA Modules:
  0.0 144.8 jit_solution(1282390263100306349)
XLA Ops:
  7.2 0.0 all-gather.4.cloned.1.call-start
  7.2 1.7 %shard_map.50 = (f32[264,256]{1,0:T(8,128)}, f32[8,64,256]{2,1,0:T(8,128)S(1)}, f32[64,256]{1,0:T(8,128)S(1)}, f32[64,128]{1,0:T(8,128)S(1)}) custom-call(f32[256,256]{1,0:T(8,128)} %rows.1, s32[1,256]{1,0:T(1,128)} %bitcast.24, f32[1,256]{1,0:T(1,128)} %bitcast.18), custom_call_target="tpu_custom_call" | custom-call | tf_op jit(solution)/shard_map/pallas_call | solution.py:290
  8.9 0.0 all-gather.4.cloned.1.call-update
  8.9 0.0 reduce-scatter.2.cloned.1.call-start
  9.0 26.7 %all_to_all.20 = f32[8,64,256]{2,1,0:T(8,128)S(1)} all-to-all(f32[8,64,256]{2,1,0:T(8,128)S(1)} %get-tuple-element.30), channel_id=1, replica_groups=mesh['z'=8,'x'=4,'yh'=4,'yl'=2,'core'=2] {'z'}, dimensions={0} | all-to-all | bytes 1048576 | tf_op jit(solution)/shard_map/all_to_all | solution.py:332
  35.6 0.0 copy-start.1
  35.6 3.1 %collective-permute-start.2 = (f32[512,256]{1,0:T(8,128)S(1)}, f32[512,256]{1,0:T(8,128)S(1)}, u32[]{:S(2)}, u32[]{:S(2)}) collective-permute-start(f32[512,256]{1,0:T(8,128)S(1)} %bitcast.12), channel_id=1, source_target_pairs={{0,16},{16,32},{32,48},{48,0},{1,17},{17,33},{33,49},{49,1},{2,18}... | collective-permute-start | bytes 1572872 | tf_op jit(solution)/shard_map/ppermute | solution.py:313
  38.8 3.4 %collective-permute-start = (f32[512,256]{1,0:T(8,128)S(1)}, f32[512,256]{1,0:T(8,128)S(1)}, u32[]{:S(2)}, u32[]{:S(2)}) collective-permute-start(f32[512,256]{1,0:T(8,128)S(1)} %bitcast.13), channel_id=1, source_target_pairs={{0,48},{16,0},{32,16},{48,32},{1,49},{17,1},{33,17},{49,33},{2,50}... | collective-permute-start | bytes 1572872 | tf_op jit(solution)/shard_map/ppermute | solution.py:313
  42.1 3.4 %collective-permute-start.1 = (f32[512,256]{1,0:T(8,128)S(1)}, f32[512,256]{1,0:T(8,128)S(1)}, u32[]{:S(2)}, u32[]{:S(2)}) collective-permute-start(f32[512,256]{1,0:T(8,128)S(1)} %bitcast.14), channel_id=1, source_target_pairs={{0,32},{16,48},{32,0},{48,16},{1,33},{17,49},{33,1},{49,17},{2,34}... | collective-permute-start | bytes 1572872 | tf_op jit(solution)/shard_map/ppermute | solution.py:313
  45.6 8.1 %all-gather.4.cloned.1.call-done = f32[1056,256]{1,0:T(8,128)} async-done(((f32[264,256]{1,0:T(8,128)}), f32[1056,256]{1,0:T(8,128)}) %all-gather.4.cloned.1.call-update) | async-done | bytes 1081360 | tf_op jit(solution)/shard_map/all_gather | solution.py:333
  53.7 0.0 copy-start
  53.7 1.2 copy-done
  54.9 0.5 shard_map.51
  55.5 3.0 %shard_map.52 = (bf16[1024,512]{1,0:T(8,128)(2,1)}, bf16[1024,512]{1,0:T(8,128)(2,1)}, f32[4,128]{1,0:T(4,128)S(1)}, f32[1024,128]{1,0:T(8,128)S(1)}, f32[1024,256]{1,0:T(8,128)S(1)}) custom-call(bf16[1024,256]{1,0:T(8,128)(2,1)S(1)} %get-tuple-element.28.refs_0_.row_high, bf16[1024,256]{1,0:T(8,128)(2,1)S(1)} %get-tuple-element.29.refs_1_.row_low, ...), custom_call_target="tpu_custom_call" | custom-call | flops 1610612736 | bytes 3670016 | tf_op jit(solution)/shard_map/pallas_call | solution.py:290
  58.5 0.0 copy-done.1
  58.5 0.0 collective-permute-done.2.refs_2_.cols_1.refs_9_
  58.5 0.0 copy-start.2
  58.5 0.0 copy-start.6
  58.5 2.8 %shard_map.53 = (bf16[1024,512]{1,0:T(8,128)(2,1)}, bf16[1024,512]{1,0:T(8,128)(2,1)}, f32[4,128]{1,0:T(4,128)S(1)}, f32[1024,128]{1,0:T(8,128)S(1)}, f32[1024,256]{1,0:T(8,128)S(1)}) custom-call(bf16[1024,256]{1,0:T(8,128)(2,1)S(1)} %get-tuple-element.28.refs_0_.row_high, bf16[1024,256]{1,0:T(8,128)(2,1)S(1)} %get-tuple-element.29.refs_1_.row_low, ...), custom_call_target="tpu_custom_call" | custom-call | flops 1610612736 | bytes 3670016 | tf_op jit(solution)/shard_map/pallas_call | solution.py:290
  61.4 0.0 copy-done.2
  61.4 0.0 collective-permute-done.cols_2.refs_10_
  61.4 0.0 copy-start.3
  61.4 0.5 collective-permute-done.1.cols_3.refs_11_
  61.9 0.0 copy-start.4
  61.9 0.0 copy-done.6
  61.9 6.1 %shard_map.54 = (bf16[1024,512]{1,0:T(8,128)(2,1)}, bf16[1024,512]{1,0:T(8,128)(2,1)}, bf16[1024,512]{1,0:T(8,128)(2,1)}, bf16[1024,512]{1,0:T(8,128)(2,1)}, f32...) custom-call(bf16[1024,256]{1,0:T(8,128)(2,1)S(1)} %get-tuple-element.28.refs_0_.row_high, ...), custom_call_target="tpu_custom_call" | custom-call | flops 3221225472 | bytes 6291456 | tf_op jit(solution)/shard_map/pallas_call | solution.py:290
  68.1 0.0 copy-done.3
  68.1 0.0 copy-done.4
  68.1 0.0 reduce-scatter.2.cloned.1.call-update
  68.1 9.1 %all-to-all-start.1 = ((f32[32,24,128]{2,1,0:T(8,128)}), f32[32,24,128]{2,1,0:T(8,128)S(1)}, u32[]{:S(2)}, u32[]{:S(2)}) async-start(f32[32,24,128]{2,1,0:T(8,128)} %get-tuple-element.38), calls=%async_computation.1 | async-start | bytes 786432 | tf_op jit(solution)/shard_map/all_to_all | solution.py:377
  77.3 5.0 %shard_map.55.refs_12_ = f32[1024,256]{1,0:T(8,128)} custom-call(f32[512,256]{1,0:T(8,128)} %bitcast.16, f32[512,256]{1,0:T(8,128)} %copy-done.2, f32[512,256]{1,0:T(8,128)} %copy-done.3, f32[512,256]{1,0:T(8,128)} %copy-done.4, f32[4,264,256]{2,1,0:T(8,128)} %bitcast.9), custom_call_target="tpu_custom_call" | custom-call | flops 2147483648 | bytes 11534336 | tf_op jit(solution)/shard_map/pallas_call | solution.py:290
  82.2 8.5 %all-to-all-done.1.message = f32[32,24,128]{2,1,0:T(8,128)S(1)} async-done(((f32[32,24,128]{2,1,0:T(8,128)}), f32[32,24,128]{2,1,0:T(8,128)S(1)}, u32[]{:S(2)}, u32[]{:S(2)}) %all-to-all-start.1) | async-done | bytes 393248 | tf_op jit(solution)/shard_map/all_to_all | solution.py:377
  90.8 7.1 %shard_map.56 = (f32[2,4,2,64,256]{4,3,2,1,0:T(8,128)S(1)}, f32[1,128]{1,0:T(1,128)S(1)}) custom-call(f32[32,24,128]{2,1,0:T(8,128)S(1)} %all-to-all-done.1.message, bf16[1024,512]{1,0:T(8,128)(2,1)} %get-tuple-element.39.refs_0_, bf16[1024,512]{1,0:T(8,128)(2,1)} %get-tuple-element.40.refs_1_, bf16[1024,512]{1,0:T(8,128)(2,1)} %get-tuple-element.41.refs_2_, ...), custom_call_target="tpu_custom_call" | custom-call | flops 3221225472 | bytes 11534336 | tf_op jit(solution)/shard_map/pallas_call | solution.py:290
  97.9 7.0 %all_to_all.21 = f32[2,4,2,64,256]{4,3,2,1,0:T(8,128)S(1)} all-to-all(f32[2,4,2,64,256]{4,3,2,1,0:T(8,128)S(1)} %get-tuple-element.47), channel_id=1, replica_groups=mesh['z'=8,'x'=4,'yh'=4,'yl'=2,'core'=2] {'core'}, dimensions={0} | all-to-all | bytes 2097152 | tf_op jit(solution)/shard_map/all_to_all | solution.py:401
  104.9 0.9 reduce_sum.9
  105.8 5.3 %all-to-all-start.3 = ((f32[8,64,256]{2,1,0:T(8,128)}), f32[8,64,256]{2,1,0:T(8,128)S(1)}, u32[]{:S(2)}, u32[]{:S(2)}) async-start(f32[8,64,256]{2,1,0:T(8,128)} %bitcast.5), calls=%async_computation.3 | async-start | bytes 1048576 | tf_op jit(solution)/shard_map/all_to_all | solution.py:402
  111.1 0.0 reduce-scatter.2.cloned.1.call-done.here
  111.2 2.6 %collective-permute-start.3 = (f32[144,256]{1,0:T(8,128)}, f32[144,256]{1,0:T(8,128)S(1)}, u32[]{:S(2)}, u32[]{:S(2)}) collective-permute-start(f32[144,256]{1,0:T(8,128)} %reduce-scatter.2.cloned.1.call-done.here), channel_id=1, source_target_pairs={{0,1},{1,0},{2,3},{3,2},{4,5},{5,4},{6,7},{7,6},{8,9},{9,8},{10,11... | collective-permute-start | bytes 442376 | tf_op jit(solution)/shard_map/ppermute | solution.py:376
  113.7 15.4 %all-to-all-done.3.parts = f32[8,64,256]{2,1,0:T(8,128)S(1)} async-done(((f32[8,64,256]{2,1,0:T(8,128)}), f32[8,64,256]{2,1,0:T(8,128)S(1)}, u32[]{:S(2)}, u32[]{:S(2)}) %all-to-all-start.3) | async-done | bytes 524320 | tf_op jit(solution)/shard_map/all_to_all | solution.py:402
  129.1 0.0 collective-permute-done.3.there
  129.1 0.0 copy-start.5
  129.1 0.9 copy-done.5
  130.0 0.3 shard_map.57
  130.3 6.2 %all-gather.1 = f32[288,256]{1,0:T(8,128)S(1)} all-gather(f32[72,256]{1,0:T(8,128)S(1)} %shard_map.57), channel_id=3, replica_groups=mesh['z'=8,'x'=4,'yh'=4,'yl'=2,'core'=2] {'yl','core'}, dimensions={0}, use_global_device_ids=true | all-gather | bytes 368640 | tf_op jit(solution)/shard_map/all_gather | solution.py:409
  136.5 0.7 slice.9
  137.3 0.6 reshape_squeeze.3
  (1 shorter events, 0.0 us)
Async XLA Ops:
  7.2 46.5 %all-gather.4.cloned.1.call-start = ((), (), s32[]{:S(2)}) async-start(), calls=%async_computation.6 | async-start | bytes 1351680 | tf_op jit(solution)/shard_map/all_gather | solution.py:333
  8.9 102.2 %reduce-scatter.2.cloned.1.call-start = ((), (), s32[]{:S(2)}) async-start(), calls=%async_computation.5 | async-start | bytes 1327104 | tf_op jit(solution)/shard_map/reduce_scatter | solution.py:375
  35.6 22.9 %copy-start.1 = (f32[8,64,256]{2,1,0:T(8,128)}, f32[8,64,256]{2,1,0:T(8,128)S(1)}, u32[]{:S(2)}) copy-start(f32[8,64,256]{2,1,0:T(8,128)S(1)} %all_to_all.20) | copy-start | bytes 1572868
  35.6 22.9 %collective-permute-start.2 = (f32[512,256]{1,0:T(8,128)S(1)}, f32[512,256]{1,0:T(8,128)S(1)}, u32[]{:S(2)}, u32[]{:S(2)}) collective-permute-start(f32[512,256]{1,0:T(8,128)S(1)} %bitcast.12), channel_id=1, source_target_pairs={{0,16},{16,32},{32,48},{48,0},{1,17},{17,33},{33,49},{49,1},{2,18}... | collective-permute-start | bytes 1572872 | tf_op jit(solution)/shard_map/ppermute | solution.py:313
  38.8 22.6 %collective-permute-start = (f32[512,256]{1,0:T(8,128)S(1)}, f32[512,256]{1,0:T(8,128)S(1)}, u32[]{:S(2)}, u32[]{:S(2)}) collective-permute-start(f32[512,256]{1,0:T(8,128)S(1)} %bitcast.13), channel_id=1, source_target_pairs={{0,48},{16,0},{32,16},{48,32},{1,49},{17,1},{33,17},{49,33},{2,50}... | collective-permute-start | bytes 1572872 | tf_op jit(solution)/shard_map/ppermute | solution.py:313
  42.1 19.8 %collective-permute-start.1 = (f32[512,256]{1,0:T(8,128)S(1)}, f32[512,256]{1,0:T(8,128)S(1)}, u32[]{:S(2)}, u32[]{:S(2)}) collective-permute-start(f32[512,256]{1,0:T(8,128)S(1)} %bitcast.14), channel_id=1, source_target_pairs={{0,32},{16,48},{32,0},{48,16},{1,33},{17,49},{33,1},{49,17},{2,34}... | collective-permute-start | bytes 1572872 | tf_op jit(solution)/shard_map/ppermute | solution.py:313
  53.7 1.2 copy-start
  58.5 2.9 %copy-start.2 = (f32[512,256]{1,0:T(8,128)}, f32[512,256]{1,0:T(8,128)S(1)}, u32[]{:S(2)}) copy-start(f32[512,256]{1,0:T(8,128)S(1)} %collective-permute-done.2.refs_2_.cols_1.refs_9_) | copy-start | bytes 1572868
  58.5 3.4 %copy-start.6 = (f32[256]{0:T(256)S(1)}, f32[256]{0:T(256)}, u32[]{:S(2)}) copy-start(f32[256]{0:T(256)} %param.5) | copy-start | bytes 3076
  61.4 6.7 %copy-start.3 = (f32[512,256]{1,0:T(8,128)}, f32[512,256]{1,0:T(8,128)S(1)}, u32[]{:S(2)}) copy-start(f32[512,256]{1,0:T(8,128)S(1)} %collective-permute-done.cols_2.refs_10_) | copy-start | bytes 1572868
  61.9 6.2 %copy-start.4 = (f32[512,256]{1,0:T(8,128)}, f32[512,256]{1,0:T(8,128)S(1)}, u32[]{:S(2)}) copy-start(f32[512,256]{1,0:T(8,128)S(1)} %collective-permute-done.1.cols_3.refs_11_) | copy-start | bytes 1572868
  68.1 22.7 %all-to-all-start.1 = ((f32[32,24,128]{2,1,0:T(8,128)}), f32[32,24,128]{2,1,0:T(8,128)S(1)}, u32[]{:S(2)}, u32[]{:S(2)}) async-start(f32[32,24,128]{2,1,0:T(8,128)} %get-tuple-element.38), calls=%async_computation.1 | async-start | bytes 786432 | tf_op jit(solution)/shard_map/all_to_all | solution.py:377
  105.8 23.3 %all-to-all-start.3 = ((f32[8,64,256]{2,1,0:T(8,128)}), f32[8,64,256]{2,1,0:T(8,128)S(1)}, u32[]{:S(2)}, u32[]{:S(2)}) async-start(f32[8,64,256]{2,1,0:T(8,128)} %bitcast.5), calls=%async_computation.3 | async-start | bytes 1048576 | tf_op jit(solution)/shard_map/all_to_all | solution.py:402
  111.2 17.9 %collective-permute-start.3 = (f32[144,256]{1,0:T(8,128)}, f32[144,256]{1,0:T(8,128)S(1)}, u32[]{:S(2)}, u32[]{:S(2)}) collective-permute-start(f32[144,256]{1,0:T(8,128)} %reduce-scatter.2.cloned.1.call-done.here), channel_id=1, source_target_pairs={{0,1},{1,0},{2,3},{3,2},{4,5},{5,4},{6,7},{7,6},{8,9},{9,8},{10,11... | collective-permute-start | bytes 442376 | tf_op jit(solution)/shard_map/ppermute | solution.py:376
  129.1 0.9 copy-start.5
Sparse Core Ops, SparseCore 0:
  10.1 43.5 all-gather.3
  68.2 38.4 reduce-scatter.1

commit v4 on v3

--- a/solution.py
+++ b/solution.py
@@ -151,8 +151,8 @@
 
 
 def last_kernel(
-    row_high, row_low, cols_2, cols_3, partner, hits, plain, cotangent, sums_0, sums_1, high_2,
-    low_2, high_3, low_3, told, shared, *refs,
+    row_high, row_low, cols_2, cols_3, partner, hits, cotangent, sums_0, sums_1, high_2, low_2,
+    high_3, low_3, told, hits_out, *refs,
 ):
     *held, sums, sems = refs
     count = cols_2.shape[0]
@@ -161,24 +161,14 @@
     copies, totals = [], [None, None]
     for block in range(row_high.shape[0] // tile):
         at = slice(block * tile, (block + 1) * tile)
-        summed, hit = plain[at, :], hits[at, :]
+        hit = hits[at, :]
         for i in range(2):
             exps, total, more = score(2 + i, at, row_high, row_low, parts[i], partner, count)
             totals[i] = total if block == 0 else totals[i] + total
-            exp_parts = halves(exps)
             ends = slice(2 * i, 2 * i + 2)
-            copies += send_parts(sems.at[block * 2 + i], at, exp_parts, held[ends], outs[ends])
-            summed += products(exp_parts, parts[i])
+            copies += send_parts(sems.at[block * 2 + i], at, halves(exps), held[ends], outs[ends])
             hit += more
-        for part in range(tile // lanes):
-            turned = jnp.transpose(hit[part * lanes : (part + 1) * lanes, :])
-            row = math.log(2.0) * jnp.sum(turned, axis=0, keepdims=True)
-            for side in range(2):
-                k = block * 4 + part * 2 + side
-                shared[k, :quarter, :] = summed[(part * 2 + side) * 64 : (part * 2 + side + 1) * 64]
-                shared[k, quarter:, :] = jnp.zeros((8, shared.shape[2]), f32)
-                here = row if side == 0 else pltpu.roll(row, 64, 1)
-                shared[k, quarter : quarter + 1, :lanes] = here
+        hits_out[at, :] = hit
     own = cotangent[pl.ds(lax.axis_index("yl"), 1), :]
     own = jnp.where(lax.axis_index("core") == 0, own, pltpu.roll(own, 64, 1))
     late = [jnp.concatenate(pieces(total), axis=0) for total in totals]
@@ -191,7 +181,47 @@
     wait_all(copies)
 
 
-def shadow_kernel(cols_0, cols_1, cols_2, cols_3, rows, out, cols_in, info, paired_rows, sems):
+def share_kernel(
+    high_2, low_2, high_3, low_3, cols_2, cols_3, plain, hits, out, exps_in, cols_in, plain_in,
+    hits_in, shared, sems,
+):
+    first = fetch(
+        sems.at[4], (cols_2, cols_in.at[0]), (cols_3, cols_in.at[1]), (plain, plain_in),
+        (hits, hits_in),
+    )
+    arrivals = []
+    for block in range(4):
+        at = pl.ds(block * tile, tile)
+        pairs = enumerate((high_2, low_2, high_3, low_3))
+        pairs = [(ref.at[at, :], exps_in.at[i, at, :]) for i, ref in pairs]
+        arrivals.append(fetch(sems.at[block], *pairs))
+    wait_all(first)
+    parts = [halves(cols_in[i]) for i in range(2)]
+    sent = []
+    for block, arrival in enumerate(arrivals):
+        at = slice(block * tile, (block + 1) * tile)
+        wait_all(arrival)
+        summed = plain_in[at, :]
+        for i in range(2):
+            summed += products((exps_in[2 * i, at, :], exps_in[2 * i + 1, at, :]), parts[i])
+        for part in range(tile // lanes):
+            turned = hits_in[at.start + part * lanes : at.start + (part + 1) * lanes, :]
+            row = math.log(2.0) * jnp.sum(jnp.transpose(turned), axis=0, keepdims=True)
+            for side in range(2):
+                k = block * 4 + part * 2 + side
+                shared[k, :quarter, :] = summed[(part * 2 + side) * 64 : (part * 2 + side + 1) * 64]
+                shared[k, quarter:, :] = jnp.zeros((8, shared.shape[2]), f32)
+                here = row if side == 0 else pltpu.roll(row, 64, 1)
+                shared[k, quarter : quarter + 1, :lanes] = here
+        ends = pl.ds(block * 4, 4)
+        sent += fetch(sems.at[5 + block], (shared.at[ends], out.at[ends]))
+    wait_all(sent)
+
+
+def shadow_kernel(
+    cols_0, cols_1, cols_2, cols_3, rows, shared, out, cols_in, info, paired_rows, sems
+):
+    del shared
     cols = (cols_0, cols_1, cols_2, cols_3)
     copies = fetch(
         sems, *[(ref, cols_in.at[i]) for i, ref in enumerate(cols)], *info_pairs(rows, info)
@@ -215,11 +245,12 @@
     exps, cols, (paired_rows, rows) = ins[:8], ins[8:12], ins[12:]
     exps_in, refs = refs[:8], refs[8:]
     cols_in, paired_in, info, scales, weights, au_high, au_low, total, sems = refs
+    facts = fetch(sems.at[4], *info_pairs(rows, info))
     arrivals = []
     for chunk in range(4):
         pairs = [(ref, exps_in[i]) for i, ref in enumerate(exps) if i % 4 == chunk]
         arrivals.append(fetch(sems.at[chunk], (cols[chunk], cols_in.at[chunk]), *pairs))
-    last = fetch(sems.at[4], (paired_rows, paired_in), *info_pairs(rows, info))
+    last = fetch(sems.at[5], (paired_rows, paired_in))
     scales[...] = jnp.sum(message[...], axis=0)[:16, :]
     sums = []
     place = lax.broadcasted_iota(jnp.int32, (1, lanes), 1)
@@ -235,7 +266,16 @@
     own_sum[...] = jnp.where(lax.rem(z, 2) == 0, own, pltpu.roll(own, 64, 1))
     columns = jnp.transpose(jnp.concatenate([weights[...] / jnp.concatenate(sums, axis=0)] * 8, axis=0))
     count = cols_in.shape[1]
-    ids = []
+    ids = sum((pieces(seen_ids(chunk, count)) for chunk in range(4)), [])
+    wait_all(facts)
+    paired_weights = []
+    for block in range(4):
+        partner = as_column(info[block, 0:1, :]).astype(jnp.int32)
+        spread = jnp.zeros((tile, lanes), f32)
+        for i, piece in enumerate(ids):
+            spread += jnp.where(partner == piece, weights[i : i + 1, :], 0.0)
+        own_weight = as_column(info[block, 1:2, :])[:, :1]
+        paired_weights.append(own_weight + jnp.sum(spread, axis=1, keepdims=True))
     for chunk, arrival in enumerate(arrivals):
         arrival[0].wait()
         for part in range(4):
@@ -245,7 +285,6 @@
             au_high[at, :], au_low[at, :] = halves(scaled)
         at = slice(chunk * count, (chunk + 1) * count)
         scaled_cols = (au_high[at, :], au_low[at, :])
-        ids += pieces(seen_ids(chunk, count))
         wait_all(arrival[1:])
         for block in range(4):
             rows_at = slice(block * tile, (block + 1) * tile)
@@ -256,12 +295,7 @@
     wait_all(last)
     for block in range(4):
         rows_at = slice(block * tile, (block + 1) * tile)
-        partner = as_column(info[block, 0:1, :]).astype(jnp.int32)
-        spread = jnp.zeros((tile, lanes), f32)
-        for i, piece in enumerate(ids):
-            spread += jnp.where(partner == piece, weights[i : i + 1, :], 0.0)
-        weight = as_column(info[block, 1:2, :])[:, :1] + jnp.sum(spread, axis=1, keepdims=True)
-        result = total[rows_at, :] - weight * paired_in[rows_at, :]
+        result = total[rows_at, :] - paired_weights[block] * paired_in[rows_at, :]
         for part in range(4):
             out[part % 2, block, part // 2] = result[part * 64 : (part + 1) * 64]
 
@@ -361,28 +395,40 @@
         lows.append(low)
         col_sums.append(sums)
     hits, plain = before
-    high_2, low_2, high_3, low_3, told, shared = call(
+    high_2, low_2, high_3, low_3, told, hits = call(
         last_kernel,
-        exps_out * 2 + [((32, 24, lanes), f32), ((16, quarter + 8, width), f32)],
-        (row_high, row_low, *cols[2:], partners, hits, plain, cotangent.reshape(2, lanes), *col_sums),
+        exps_out * 2 + [((32, 24, lanes), f32), ((count, lanes), f32)],
+        (row_high, row_low, *cols[2:], partners, hits, cotangent.reshape(2, lanes), *col_sums),
         32,
-        estimate(6, count, 2 * seen, width, 2 * count * seen),
+        estimate(3, count, 2 * seen, width, 2 * count * seen),
         own_exps * 2 + [pltpu.VMEM((24, lanes), f32), copies((8, 2))],
         far_outs=range(4),
     )
     highs += [high_2, high_3]
     lows += [low_2, low_3]
+    (shared,) = call(
+        share_kernel,
+        [((16, quarter + 8, width), f32)],
+        (high_2, low_2, high_3, low_3, *cols[2:], plain, hits),
+        24,
+        estimate(3, count, 2 * seen, width),
+        [pltpu.VMEM((4, count, seen), bf16), pltpu.VMEM((2, seen, width), f32), own_rows[0],
+         pltpu.VMEM((count, lanes), f32), pltpu.VMEM((16, quarter + 8, width), f32),
+         copies((9, 4))],
+        far=range(8),
+        far_outs=(0,),
+    )
     here = lax.psum_scatter(shared.reshape(-1, width), ("yh", "yl"), tiled=True)
     there = lax.ppermute(here, "core", [(0, 1), (1, 0)])
     message = lax.all_to_all(told, ("z", "x"), 0, 0, tiled=True)
     (paired_rows,) = call(
         shadow_kernel,
         row_sums[:1],
-        (*cols, rows),
+        (*cols, rows, shared),
         24,
         estimate(2, count, 4 * seen, width),
         [pltpu.VMEM((4, seen, width), f32), info, own_rows[0], copies((8,))],
-        far=range(5),
+        far=range(6),
         far_outs=(0,),
     )
     partial, own_sum = call(
@@ -390,12 +436,12 @@
         [((2, 4, 2, quarter, width), f32), ((1, lanes), f32)],
         (message, *highs, *lows, *cols, paired_rows, rows),
         28,
-        estimate(3, count, 4 * seen, width),
+        estimate(30, count, 4 * seen, width),
         own_exps * 4
         + [pltpu.VMEM((4, seen, width), f32), own_rows[0], info]
         + [pltpu.VMEM((16, lanes), f32)] * 2
         + [pltpu.VMEM((4 * seen, width), bf16)] * 2
-        + [own_rows[0], copies((5, 5))],
+        + [own_rows[0], copies((6, 4))],
         far=range(1, 15),
     )
     halved = jnp.sum(lax.all_to_all(partial, "core", 0, 0, tiled=True), axis=0)

time: 145 us -> 152 us (1.048)
  Pallas kernels: 26.6 us -> 30.5 us
  starting transfers between devices: 27 us -> 30.4 us
  waiting for transfers between devices: 32.6 us -> 29.7 us
  local copies, waits for them, and re-layouts: 3.56 us -> 5.31 us
    reduce_scatter x1, waiting for transfers between devices: 0.01 us -> 16.5 us  [per_device(): here = lax.psum_scatter(shared.reshape(-1, width), ('yh', 'yl'), tiled=True)]
    all_to_all x1, waiting for transfers between devices: 15.4 us -> 0.01 us  [per_device(): lax.all_to_all(halved.reshape(8, quarter, width), ('yh', 'yl'), 0, 0, til...]
    all_to_all x1, waiting for transfers between devices: 8.54 us -> 1.56 us  [per_device(): message = lax.all_to_all(told, ('z', 'x'), 0, 0, tiled=True)]
    ppermute x1, starting transfers between devices: 2.56 us -> 6.76 us  [per_device(): there = lax.ppermute(here, 'core', [(0, 1), (1, 0)])]
    pallas_call x8 -> x9, Pallas kernels: 26.6 us -> 30.5 us  [call(): pl.pallas_call(kernel, in_specs=[anywhere if i in far else vmem for i in...]
    all_to_all x1, starting transfers between devices: 9.14 us -> 6.6 us  [per_device(): message = lax.all_to_all(told, ('z', 'x'), 0, 0, tiled=True)]
    ppermute x3, waiting for transfers between devices: 0.51 us -> 2.86 us  [passed_along(): return lax.ppermute(array, 'x', [(i, (i + by) % 4) for i in range(4)])]
    unnamed x14 -> x18, local copies, waits for them, and re-layouts: 2.17 us -> 3.93 us
  transfers between devices with their start and end apart: 8 -> 8, of which waited for: 4 -> 5; matrix products, arithmetic and copies ran while one was open for 1% -> 1% of each run, Pallas kernels for 13% -> 16%
where the time goes in v4:
time: 152 us
  blocking collectives  40.5 us (27%)
  Pallas kernels  30.5 us (20%)
  starting transfers between devices  30.4 us (20%)
  waiting for transfers between devices  29.7 us (20%)
  between operations  14.2 us (9%)
  local copies, waits for them, and re-layouts  5.31 us (3%)
    pallas_call x9, Pallas kernels, call(): pl.pallas_call(kernel, in_specs=[anywhere if i in far else vmem for i in...  30.5 us
    all_to_all x1, blocking collectives, per_device(): here = lax.all_to_all(told, 'z', 0, 0, tiled=True).reshape(seen, width)  26.7 us
    reduce_scatter x1, waiting for transfers between devices, per_device(): here = lax.psum_scatter(shared.reshape(-1, width), ('yh', 'yl'), tiled=True)  16.5 us
    ppermute x3, starting transfers between devices, passed_along(): return lax.ppermute(array, 'x', [(i, (i + by) % 4) for i in range(4)])  10.5 us
    all_gather x1, waiting for transfers between devices, per_device(): rows = lax.all_gather(packed_rows, 'yh')  7.55 us
    all_to_all x1, blocking collectives, per_device(): halved = jnp.sum(lax.all_to_all(partial, 'core', 0, 0, tiled=True), axis=0)  6.97 us
    all_gather x1, blocking collectives, per_device(): result = lax.all_gather(result, ('yl', 'core'))  6.92 us
    ppermute x1, starting transfers between devices, per_device(): there = lax.ppermute(here, 'core', [(0, 1), (1, 0)])  6.76 us
  transfers between devices with their start and end apart: 8, of which 5 were waited for; matrix products, arithmetic and copies ran while one was open for 1% of the time, Pallas kernels for 16%

profile of v4, /device:TPU:1, one launch (start us, length us, event | category | flops | bytes accessed | tf_op | source)
XLA Modules:
  0.0 151.6 jit_solution(3905021908790113370)
XLA Ops:
  7.2 0.0 all-gather.4.cloned.1.call-start
  7.2 1.7 %shard_map.50 = (f32[264,256]{1,0:T(8,128)}, f32[8,64,256]{2,1,0:T(8,128)S(1)}, f32[64,256]{1,0:T(8,128)S(1)}, f32[64,128]{1,0:T(8,128)S(1)}) custom-call(f32[256,256]{1,0:T(8,128)} %rows.1, s32[1,256]{1,0:T(1,128)} %bitcast.25, f32[1,256]{1,0:T(1,128)} %bitcast.18), custom_call_target="tpu_custom_call" | custom-call | tf_op jit(solution)/shard_map/pallas_call | solution.py:324
  8.9 0.0 all-gather.4.cloned.1.call-update
  8.9 26.7 %all_to_all.20 = f32[8,64,256]{2,1,0:T(8,128)S(1)} all-to-all(f32[8,64,256]{2,1,0:T(8,128)S(1)} %get-tuple-element.30), channel_id=1, replica_groups=mesh['z'=8,'x'=4,'yh'=4,'yl'=2,'core'=2] {'z'}, dimensions={0} | all-to-all | bytes 1048576 | tf_op jit(solution)/shard_map/all_to_all | solution.py:366
  35.6 0.0 copy-start.2
  35.6 3.1 %collective-permute-start.2 = (f32[512,256]{1,0:T(8,128)S(1)}, f32[512,256]{1,0:T(8,128)S(1)}, u32[]{:S(2)}, u32[]{:S(2)}) collective-permute-start(f32[512,256]{1,0:T(8,128)S(1)} %bitcast.12), channel_id=1, source_target_pairs={{0,16},{16,32},{32,48},{48,0},{1,17},{17,33},{33,49},{49,1},{2,18}... | collective-permute-start | bytes 1572872 | tf_op jit(solution)/shard_map/ppermute | solution.py:347
  38.7 4.4 %collective-permute-start.1 = (f32[512,256]{1,0:T(8,128)S(1)}, f32[512,256]{1,0:T(8,128)S(1)}, u32[]{:S(2)}, u32[]{:S(2)}) collective-permute-start(f32[512,256]{1,0:T(8,128)S(1)} %bitcast.13), channel_id=1, source_target_pairs={{0,32},{16,48},{32,0},{48,16},{1,33},{17,49},{33,1},{49,17},{2,34}... | collective-permute-start | bytes 1572872 | tf_op jit(solution)/shard_map/ppermute | solution.py:347
  43.1 3.1 %collective-permute-start = (f32[512,256]{1,0:T(8,128)S(1)}, f32[512,256]{1,0:T(8,128)S(1)}, u32[]{:S(2)}, u32[]{:S(2)}) collective-permute-start(f32[512,256]{1,0:T(8,128)S(1)} %bitcast.14), channel_id=1, source_target_pairs={{0,48},{16,0},{32,16},{48,32},{1,49},{17,1},{33,17},{49,33},{2,50}... | collective-permute-start | bytes 1572872 | tf_op jit(solution)/shard_map/ppermute | solution.py:347
  46.1 7.6 %all-gather.4.cloned.1.call-done = f32[1056,256]{1,0:T(8,128)} async-done(((f32[264,256]{1,0:T(8,128)}), f32[1056,256]{1,0:T(8,128)}) %all-gather.4.cloned.1.call-update) | async-done | bytes 1081360 | tf_op jit(solution)/shard_map/all_gather | solution.py:367
  53.7 0.0 copy-start
  53.7 1.2 copy-done
  54.9 0.5 shard_map.51
  55.5 3.0 %shard_map.52 = (bf16[1024,512]{1,0:T(8,128)(2,1)}, bf16[1024,512]{1,0:T(8,128)(2,1)}, f32[4,128]{1,0:T(4,128)S(1)}, f32[1024,128]{1,0:T(8,128)S(1)}, f32[1024,256]{1,0:T(8,128)S(1)}) custom-call(bf16[1024,256]{1,0:T(8,128)(2,1)S(1)} %get-tuple-element.28.refs_0_.row_high, bf16[1024,256]{1,0:T(8,128)(2,1)S(1)} %get-tuple-element.29.refs_1_.row_low, ...), custom_call_target="tpu_custom_call" | custom-call | flops 1610612736 | bytes 3670016 | tf_op jit(solution)/shard_map/pallas_call | solution.py:324
  58.5 0.0 copy-done.2
  58.5 0.0 collective-permute-done.2.refs_2_.cols_1.refs_9_
  58.5 0.0 copy-start.8
  58.5 0.0 copy-start.7
  58.5 2.8 %shard_map.53 = (bf16[1024,512]{1,0:T(8,128)(2,1)}, bf16[1024,512]{1,0:T(8,128)(2,1)}, f32[4,128]{1,0:T(4,128)S(1)}, f32[1024,128]{1,0:T(8,128)S(1)}, f32[1024,256]{1,0:T(8,128)S(1)}) custom-call(bf16[1024,256]{1,0:T(8,128)(2,1)S(1)} %get-tuple-element.28.refs_0_.row_high, bf16[1024,256]{1,0:T(8,128)(2,1)S(1)} %get-tuple-element.29.refs_1_.row_low, ...), custom_call_target="tpu_custom_call" | custom-call | flops 1610612736 | bytes 3670016 | tf_op jit(solution)/shard_map/pallas_call | solution.py:324
  61.4 0.0 copy-done.8
  61.4 0.0 copy-start.1
  61.4 1.0 copy-done.1
  62.4 0.0 collective-permute-done.1.cols_3.refs_11_
  62.4 0.0 copy-start.3
  62.4 2.9 %collective-permute-done.cols_2.refs_10_ = f32[512,256]{1,0:T(8,128)S(1)} collective-permute-done((f32[512,256]{1,0:T(8,128)S(1)}, f32[512,256]{1,0:T(8,128)S(1)}, u32[]{:S(2)}, u32[]{:S(2)}) %collective-permute-start) | collective-permute-done | bytes 524320 | tf_op jit(solution)/shard_map/ppermute | solution.py:347
  65.2 0.0 copy-start.4
  65.2 0.0 copy-done.7
  65.2 3.9 %shard_map.54 = (bf16[1024,512]{1,0:T(8,128)(2,1)}, bf16[1024,512]{1,0:T(8,128)(2,1)}, bf16[1024,512]{1,0:T(8,128)(2,1)}, bf16[1024,512]{1,0:T(8,128)(2,1)}, f32...) custom-call(bf16[1024,256]{1,0:T(8,128)(2,1)S(1)} %get-tuple-element.28.refs_0_.row_high, ...), custom_call_target="tpu_custom_call" | custom-call | flops 1610612736 | bytes 6291456 | tf_op jit(solution)/shard_map/pallas_call | solution.py:324
  69.1 0.0 copy-done.3
  69.1 0.0 copy-done.4
  69.1 0.0 copy-start.5
  69.1 0.8 copy-done.5
  69.9 6.6 %all-to-all-start.1 = ((f32[32,24,128]{2,1,0:T(8,128)}), f32[32,24,128]{2,1,0:T(8,128)S(1)}, u32[]{:S(2)}, u32[]{:S(2)}) async-start(f32[32,24,128]{2,1,0:T(8,128)} %get-tuple-element.37), calls=%async_computation.1 | async-start | bytes 786432 | tf_op jit(solution)/shard_map/all_to_all | solution.py:423
  76.5 0.2 reduce-scatter.2.cloned.1.call-start
  76.8 6.9 %shard_map.55.shared = f32[16,72,256]{2,1,0:T(8,128)} custom-call(bf16[1024,512]{1,0:T(8,128)(2,1)} %get-tuple-element.40.high_2.refs_2_, bf16[1024,512]{1,0:T(8,128)(2,1)} %get-tuple-element.44.low_2.refs_6_, bf16[1024,512]{1,0:T(8,128)(2,1)} %get-tuple-element.41.high_3.refs_3_, bf16[1024,512]{1,0:T(8,128)(2,1)} %get-tuple-element.45.low_3.refs_7_, ...), custom_call_target="tpu_custom_call" | custom-call | flops 1610612736 | bytes 6291456 | tf_op jit(solution)/shard_map/pallas_call | solution.py:324
  83.7 0.0 reduce-scatter.2.cloned.1.call-update
  83.7 5.0 %shard_map.56.refs_12_ = f32[1024,256]{1,0:T(8,128)} custom-call(f32[512,256]{1,0:T(8,128)} %bitcast.16, f32[512,256]{1,0:T(8,128)} %copy-done.8, f32[512,256]{1,0:T(8,128)} %copy-done.4, f32[512,256]{1,0:T(8,128)} %copy-done.3, f32[4,264,256]{2,1,0:T(8,128)} %bitcast.9, f32[16,72,256]{2,1,0:T(8,128)} %shard_map.55.shared), custom_call_target="tpu_custom_call" | custom-call | flops 2147483648 | bytes 11534336 | tf_op jit(solution)/shard_map/pallas_call | solution.py:324
  88.7 1.6 %all-to-all-done.1.message = f32[32,24,128]{2,1,0:T(8,128)S(1)} async-done(((f32[32,24,128]{2,1,0:T(8,128)}), f32[32,24,128]{2,1,0:T(8,128)S(1)}, u32[]{:S(2)}, u32[]{:S(2)}) %all-to-all-start.1) | async-done | bytes 393248 | tf_op jit(solution)/shard_map/all_to_all | solution.py:423
  90.2 6.4 %shard_map.57 = (f32[2,4,2,64,256]{4,3,2,1,0:T(8,128)S(1)}, f32[1,128]{1,0:T(1,128)S(1)}) custom-call(f32[32,24,128]{2,1,0:T(8,128)S(1)} %all-to-all-done.1.message, bf16[1024,512]{1,0:T(8,128)(2,1)} %get-tuple-element.38.refs_0_, bf16[1024,512]{1,0:T(8,128)(2,1)} %get-tuple-element.39.refs_1_, bf16[1024,512]{1,0:T(8,128)(2,1)} %get-tuple-element.40.high_2.refs_2_, ...), custom_call_target="tpu_custom_call" | custom-call | flops 32212254720 | bytes 11534336 | tf_op jit(solution)/shard_map/pallas_call | solution.py:324
  96.6 7.0 %all_to_all.21 = f32[2,4,2,64,256]{4,3,2,1,0:T(8,128)S(1)} all-to-all(f32[2,4,2,64,256]{4,3,2,1,0:T(8,128)S(1)} %get-tuple-element.48), channel_id=1, replica_groups=mesh['z'=8,'x'=4,'yh'=4,'yl'=2,'core'=2] {'core'}, dimensions={0} | all-to-all | bytes 2097152 | tf_op jit(solution)/shard_map/all_to_all | solution.py:447
  103.6 0.9 reduce_sum.9
  104.5 6.3 %all-to-all-start.3 = ((f32[8,64,256]{2,1,0:T(8,128)}), f32[8,64,256]{2,1,0:T(8,128)S(1)}, u32[]{:S(2)}, u32[]{:S(2)}) async-start(f32[8,64,256]{2,1,0:T(8,128)} %bitcast.5), calls=%async_computation.3 | async-start | bytes 1048576 | tf_op jit(solution)/shard_map/all_to_all | solution.py:448
  110.8 16.5 %reduce-scatter.2.cloned.1.call-done.here = f32[144,256]{1,0:T(8,128)} async-done(((f32[1152,256]{1,0:T(8,128)}), f32[144,256]{1,0:T(8,128)}) %reduce-scatter.2.cloned.1.call-update) | async-done | bytes 147472 | tf_op jit(solution)/shard_map/reduce_scatter | solution.py:421
  127.2 6.8 %collective-permute-start.3 = (f32[144,256]{1,0:T(8,128)}, f32[144,256]{1,0:T(8,128)S(1)}, u32[]{:S(2)}, u32[]{:S(2)}) collective-permute-start(f32[144,256]{1,0:T(8,128)} %reduce-scatter.2.cloned.1.call-done.here), channel_id=1, source_target_pairs={{0,1},{1,0},{2,3},{3,2},{4,5},{5,4},{6,7},{7,6},{8,9},{9,8},{10,11... | collective-permute-start | bytes 442376 | tf_op jit(solution)/shard_map/ppermute | solution.py:422
  134.0 0.0 all-to-all-done.3.parts
  134.0 1.2 collective-permute-done.3.there
  135.2 0.0 copy-start.6
  135.2 0.9 copy-done.6
  136.1 0.3 shard_map.58
  136.4 6.9 %all-gather.1 = f32[288,256]{1,0:T(8,128)S(1)} all-gather(f32[72,256]{1,0:T(8,128)S(1)} %shard_map.58), channel_id=3, replica_groups=mesh['z'=8,'x'=4,'yh'=4,'yl'=2,'core'=2] {'yl','core'}, dimensions={0}, use_global_device_ids=true | all-gather | bytes 368640 | tf_op jit(solution)/shard_map/all_gather | solution.py:455
  143.4 0.7 slice.9
  144.1 0.6 reshape_squeeze.3
  (1 shorter events, 0.0 us)
Async XLA Ops:
  7.2 46.5 %all-gather.4.cloned.1.call-start = ((), (), s32[]{:S(2)}) async-start(), calls=%async_computation.6 | async-start | bytes 1351680 | tf_op jit(solution)/shard_map/all_gather | solution.py:367
  35.6 22.9 %copy-start.2 = (f32[8,64,256]{2,1,0:T(8,128)}, f32[8,64,256]{2,1,0:T(8,128)S(1)}, u32[]{:S(2)}) copy-start(f32[8,64,256]{2,1,0:T(8,128)S(1)} %all_to_all.20) | copy-start | bytes 1572868
  35.6 22.9 %collective-permute-start.2 = (f32[512,256]{1,0:T(8,128)S(1)}, f32[512,256]{1,0:T(8,128)S(1)}, u32[]{:S(2)}, u32[]{:S(2)}) collective-permute-start(f32[512,256]{1,0:T(8,128)S(1)} %bitcast.12), channel_id=1, source_target_pairs={{0,16},{16,32},{32,48},{48,0},{1,17},{17,33},{33,49},{49,1},{2,18}... | collective-permute-start | bytes 1572872 | tf_op jit(solution)/shard_map/ppermute | solution.py:347
  38.7 23.7 %collective-permute-start.1 = (f32[512,256]{1,0:T(8,128)S(1)}, f32[512,256]{1,0:T(8,128)S(1)}, u32[]{:S(2)}, u32[]{:S(2)}) collective-permute-start(f32[512,256]{1,0:T(8,128)S(1)} %bitcast.13), channel_id=1, source_target_pairs={{0,32},{16,48},{32,0},{48,16},{1,33},{17,49},{33,1},{49,17},{2,34}... | collective-permute-start | bytes 1572872 | tf_op jit(solution)/shard_map/ppermute | solution.py:347
  43.1 22.2 %collective-permute-start = (f32[512,256]{1,0:T(8,128)S(1)}, f32[512,256]{1,0:T(8,128)S(1)}, u32[]{:S(2)}, u32[]{:S(2)}) collective-permute-start(f32[512,256]{1,0:T(8,128)S(1)} %bitcast.14), channel_id=1, source_target_pairs={{0,48},{16,0},{32,16},{48,32},{1,49},{17,1},{33,17},{49,33},{2,50}... | collective-permute-start | bytes 1572872 | tf_op jit(solution)/shard_map/ppermute | solution.py:347
  53.7 1.2 copy-start
  58.5 2.9 %copy-start.8 = (f32[512,256]{1,0:T(8,128)}, f32[512,256]{1,0:T(8,128)S(1)}, u32[]{:S(2)}) copy-start(f32[512,256]{1,0:T(8,128)S(1)} %collective-permute-done.2.refs_2_.cols_1.refs_9_) | copy-start | bytes 1572868
  58.5 6.7 %copy-start.7 = (f32[256]{0:T(256)S(1)}, f32[256]{0:T(256)}, u32[]{:S(2)}) copy-start(f32[256]{0:T(256)} %param.5) | copy-start | bytes 3076
  61.4 1.0 copy-start.1
  62.4 6.7 %copy-start.3 = (f32[512,256]{1,0:T(8,128)}, f32[512,256]{1,0:T(8,128)S(1)}, u32[]{:S(2)}) copy-start(f32[512,256]{1,0:T(8,128)S(1)} %collective-permute-done.1.cols_3.refs_11_) | copy-start | bytes 1572868
  65.2 3.9 %copy-start.4 = (f32[512,256]{1,0:T(8,128)}, f32[512,256]{1,0:T(8,128)S(1)}, u32[]{:S(2)}) copy-start(f32[512,256]{1,0:T(8,128)S(1)} %collective-permute-done.cols_2.refs_10_) | copy-start | bytes 1572868
  69.1 0.8 copy-start.5
  69.9 20.3 %all-to-all-start.1 = ((f32[32,24,128]{2,1,0:T(8,128)}), f32[32,24,128]{2,1,0:T(8,128)S(1)}, u32[]{:S(2)}, u32[]{:S(2)}) async-start(f32[32,24,128]{2,1,0:T(8,128)} %get-tuple-element.37), calls=%async_computation.1 | async-start | bytes 786432 | tf_op jit(solution)/shard_map/all_to_all | solution.py:423
  76.5 50.7 %reduce-scatter.2.cloned.1.call-start = ((), (), s32[]{:S(2)}) async-start(), calls=%async_computation.5 | async-start | bytes 1327104 | tf_op jit(solution)/shard_map/reduce_scatter | solution.py:421
  104.5 29.6 %all-to-all-start.3 = ((f32[8,64,256]{2,1,0:T(8,128)}), f32[8,64,256]{2,1,0:T(8,128)S(1)}, u32[]{:S(2)}, u32[]{:S(2)}) async-start(f32[8,64,256]{2,1,0:T(8,128)} %bitcast.5), calls=%async_computation.3 | async-start | bytes 1048576 | tf_op jit(solution)/shard_map/all_to_all | solution.py:448
  127.2 8.0 %collective-permute-start.3 = (f32[144,256]{1,0:T(8,128)}, f32[144,256]{1,0:T(8,128)S(1)}, u32[]{:S(2)}, u32[]{:S(2)}) collective-permute-start(f32[144,256]{1,0:T(8,128)} %reduce-scatter.2.cloned.1.call-done.here), channel_id=1, source_target_pairs={{0,1},{1,0},{2,3},{3,2},{4,5},{5,4},{6,7},{7,6},{8,9},{9,8},{10,11... | collective-permute-start | bytes 442376 | tf_op jit(solution)/shard_map/ppermute | solution.py:422
  135.2 0.9 copy-start.6
Sparse Core Ops, SparseCore 0:
  10.1 43.5 all-gather.3
  83.8 43.3 reduce-scatter.1

commit v5 on v3

--- a/solution.py
+++ b/solution.py
@@ -152,9 +152,9 @@
 
 def last_kernel(
     row_high, row_low, cols_2, cols_3, partner, hits, plain, cotangent, sums_0, sums_1, high_2,
-    low_2, high_3, low_3, told, shared, *refs,
+    low_2, high_3, low_3, told, shared_out, *refs,
 ):
-    *held, sums, sems = refs
+    *held, sums, shared, sems, shared_sems = refs
     count = cols_2.shape[0]
     outs = (high_2, low_2, high_3, low_3)
     parts = [halves(cols_2[...]), halves(cols_3[...])]
@@ -179,6 +179,8 @@
                 shared[k, quarter:, :] = jnp.zeros((8, shared.shape[2]), f32)
                 here = row if side == 0 else pltpu.roll(row, 64, 1)
                 shared[k, quarter : quarter + 1, :lanes] = here
+        ends = pl.ds(block * 4, 4)
+        copies += fetch(shared_sems.at[block], (shared.at[ends], shared_out.at[ends]))
     own = cotangent[pl.ds(lax.axis_index("yl"), 1), :]
     own = jnp.where(lax.axis_index("core") == 0, own, pltpu.roll(own, 64, 1))
     late = [jnp.concatenate(pieces(total), axis=0) for total in totals]
@@ -215,11 +217,12 @@
     exps, cols, (paired_rows, rows) = ins[:8], ins[8:12], ins[12:]
     exps_in, refs = refs[:8], refs[8:]
     cols_in, paired_in, info, scales, weights, au_high, au_low, total, sems = refs
+    facts = fetch(sems.at[4], *info_pairs(rows, info))
     arrivals = []
     for chunk in range(4):
         pairs = [(ref, exps_in[i]) for i, ref in enumerate(exps) if i % 4 == chunk]
         arrivals.append(fetch(sems.at[chunk], (cols[chunk], cols_in.at[chunk]), *pairs))
-    last = fetch(sems.at[4], (paired_rows, paired_in), *info_pairs(rows, info))
+    last = fetch(sems.at[5], (paired_rows, paired_in))
     scales[...] = jnp.sum(message[...], axis=0)[:16, :]
     sums = []
     place = lax.broadcasted_iota(jnp.int32, (1, lanes), 1)
@@ -235,7 +238,16 @@
     own_sum[...] = jnp.where(lax.rem(z, 2) == 0, own, pltpu.roll(own, 64, 1))
     columns = jnp.transpose(jnp.concatenate([weights[...] / jnp.concatenate(sums, axis=0)] * 8, axis=0))
     count = cols_in.shape[1]
-    ids = []
+    ids = sum((pieces(seen_ids(chunk, count)) for chunk in range(4)), [])
+    wait_all(facts)
+    paired_weights = []
+    for block in range(4):
+        partner = as_column(info[block, 0:1, :]).astype(jnp.int32)
+        spread = jnp.zeros((tile, lanes), f32)
+        for i, piece in enumerate(ids):
+            spread += jnp.where(partner == piece, weights[i : i + 1, :], 0.0)
+        own_weight = as_column(info[block, 1:2, :])[:, :1]
+        paired_weights.append(own_weight + jnp.sum(spread, axis=1, keepdims=True))
     for chunk, arrival in enumerate(arrivals):
         arrival[0].wait()
         for part in range(4):
@@ -245,7 +257,6 @@
             au_high[at, :], au_low[at, :] = halves(scaled)
         at = slice(chunk * count, (chunk + 1) * count)
         scaled_cols = (au_high[at, :], au_low[at, :])
-        ids += pieces(seen_ids(chunk, count))
         wait_all(arrival[1:])
         for block in range(4):
             rows_at = slice(block * tile, (block + 1) * tile)
@@ -256,27 +267,26 @@
     wait_all(last)
     for block in range(4):
         rows_at = slice(block * tile, (block + 1) * tile)
-        partner = as_column(info[block, 0:1, :]).astype(jnp.int32)
-        spread = jnp.zeros((tile, lanes), f32)
-        for i, piece in enumerate(ids):
-            spread += jnp.where(partner == piece, weights[i : i + 1, :], 0.0)
-        weight = as_column(info[block, 1:2, :])[:, :1] + jnp.sum(spread, axis=1, keepdims=True)
-        result = total[rows_at, :] - weight * paired_in[rows_at, :]
+        result = total[rows_at, :] - paired_weights[block] * paired_in[rows_at, :]
         for part in range(4):
             out[part % 2, block, part // 2] = result[part * 64 : (part + 1) * 64]
 
 
-def final_kernel(parts, here, there, own_sum, cotangent, unit, norms, out):
+def losses_kernel(here, there, own_sum, cotangent, scaled, losses):
     mine = pl.ds(pl.multiple_of(lax.axis_index("core") * (quarter + 8), 8), quarter + 8)
     shared = here[mine, :] + there[mine, :]
     own = cotangent[pl.ds(lax.axis_index("yl"), 1), :]
     own = jnp.where(lax.axis_index("core") == 0, own, pltpu.roll(own, 64, 1))
-    scale = as_column(own / own_sum[...])[:quarter, :1]
-    grad = inv_temp * (jnp.sum(parts[...], axis=0) + scale * shared[:quarter, :])
+    scaled[...] = as_column(own / own_sum[...])[:quarter, :1] * shared[:quarter, :]
+    row = jnp.log(own_sum[...]) - shared[quarter : quarter + 1, :lanes]
+    losses[...] = jnp.broadcast_to(row, losses.shape)
+
+
+def final_kernel(parts, scaled, unit, norms, losses, out):
+    del losses
+    grad = inv_temp * (jnp.sum(parts[...], axis=0) + scaled[...])
     along = jnp.sum(unit[...] * grad, axis=1, keepdims=True)
-    out[:quarter, :] = (grad - unit[...] * along) / norms[:, :1]
-    out[quarter:, :] = jnp.zeros((8, out.shape[1]), f32)
-    out[quarter : quarter + 1, :lanes] = jnp.log(own_sum[...]) - shared[quarter : quarter + 1, :lanes]
+    out[...] = (grad - unit[...] * along) / norms[:, :1]
 
 
 vmem, anywhere = pl.BlockSpec(memory_space=pltpu.VMEM), pl.BlockSpec(memory_space=pl.ANY)
@@ -367,8 +377,10 @@
         (row_high, row_low, *cols[2:], partners, hits, plain, cotangent.reshape(2, lanes), *col_sums),
         32,
         estimate(6, count, 2 * seen, width, 2 * count * seen),
-        own_exps * 2 + [pltpu.VMEM((24, lanes), f32), copies((8, 2))],
-        far_outs=range(4),
+        own_exps * 2
+        + [pltpu.VMEM((24, lanes), f32), pltpu.VMEM((16, quarter + 8, width), f32)]
+        + [copies((8, 2)), copies((4, 1))],
+        far_outs=(0, 1, 2, 3, 5),
     )
     highs += [high_2, high_3]
     lows += [low_2, low_3]
@@ -395,19 +407,26 @@
         + [pltpu.VMEM((4, seen, width), f32), own_rows[0], info]
         + [pltpu.VMEM((16, lanes), f32)] * 2
         + [pltpu.VMEM((4 * seen, width), bf16)] * 2
-        + [own_rows[0], copies((5, 5))],
+        + [own_rows[0], copies((6, 4))],
         far=range(1, 15),
     )
     halved = jnp.sum(lax.all_to_all(partial, "core", 0, 0, tiled=True), axis=0)
     swapped = lax.all_to_all(halved.reshape(8, quarter, width), ("yh", "yl"), 0, 0, tiled=True)
-    (result,) = call(
+    scaled, losses = call(
+        losses_kernel,
+        [((quarter, width), f32), ((8, lanes), f32)],
+        (here, there, own_sum, cotangent.reshape(2, lanes)),
+        4,
+    )
+    losses = lax.all_gather(losses, ("yl", "core"))[:, 0, :quarter].reshape(-1)
+    (grads,) = call(
         final_kernel,
-        [((quarter + 8, width), f32)],
-        (swapped, here, there, own_sum, cotangent.reshape(2, lanes), own_unit, norms),
+        [((quarter, width), f32)],
+        (swapped, scaled, own_unit, norms, losses[None]),
         4,
-    )
-    result = lax.all_gather(result, ("yl", "core"))
-    return result[:, quarter, :quarter].reshape(-1), result[:, :quarter].reshape(-1, width)
+        far=(4,),
+    )
+    return losses, lax.all_gather(grads, ("yl", "core"), tiled=True)
 
 
 def solution(mesh):

time: 145 us -> 143 us (0.986)
  waiting for transfers between devices: 32.6 us -> 19.8 us
  blocking collectives: 39.8 us -> 50.1 us
    all_to_all x1, waiting for transfers between devices: 15.4 us -> 1.37 us  [per_device(): lax.all_to_all(halved.reshape(8, quarter, width), ('yh', 'yl'), 0, 0, til...]
    all_gather x1 -> x2, blocking collectives: 6.2 us -> 16.5 us  [the longest x1 10.3 us: per_device(): losses = lax.all_gather(losses, ('yl', 'core'))[:, 0, :quarter].reshape(-1)]
    pallas_call x8 -> x9, Pallas kernels: 26.6 us -> 25.9 us  [call(): pl.pallas_call(kernel, in_specs=[anywhere if i in far else vmem for i in...]
  transfers between devices with their start and end apart: 8 -> 8, of which waited for: 4 -> 5; matrix products, arithmetic and copies ran while one was open for 1% -> 2% of each run, Pallas kernels for 13% -> 13%
where the time goes in v5:
time: 143 us; the launch traced here: 142 us
  blocking collectives  50.1 us (35%)
  starting transfers between devices  27.1 us (19%)
  Pallas kernels  25.9 us (18%)
  waiting for transfers between devices  19.8 us (14%)
  between operations  14.2 us (10%)
  local copies, waits for them, and re-layouts  4.16 us (3%)
    all_to_all x1, blocking collectives, per_device(): here = lax.all_to_all(told, 'z', 0, 0, tiled=True).reshape(seen, width)  26.7 us
    pallas_call x9, Pallas kernels, call(): pl.pallas_call(kernel, in_specs=[anywhere if i in far else vmem for i in...  25.9 us
    all_gather x1, blocking collectives, per_device(): losses = lax.all_gather(losses, ('yl', 'core'))[:, 0, :quarter].reshape(-1)  10.3 us
    ppermute x3, starting transfers between devices, passed_along(): return lax.ppermute(array, 'x', [(i, (i + by) % 4) for i in range(4)])  9.92 us
    all_to_all x1, starting transfers between devices, per_device(): message = lax.all_to_all(told, ('z', 'x'), 0, 0, tiled=True)  9.13 us
    all_to_all x1, waiting for transfers between devices, per_device(): message = lax.all_to_all(told, ('z', 'x'), 0, 0, tiled=True)  8.52 us
    all_gather x1, waiting for transfers between devices, per_device(): rows = lax.all_gather(packed_rows, 'yh')  8.11 us
    all_to_all x1, blocking collectives, per_device(): halved = jnp.sum(lax.all_to_all(partial, 'core', 0, 0, tiled=True), axis=0)  6.97 us
  transfers between devices with their start and end apart: 8, of which 5 were waited for; matrix products, arithmetic and copies ran while one was open for 2% of the time, Pallas kernels for 13%

profile of v5, /device:TPU:1, one launch (start us, length us, event | category | flops | bytes accessed | tf_op | source)
XLA Modules:
  0.0 142.2 jit_solution(16971511667463193850)
XLA Ops:
  7.2 0.0 all-gather.4.cloned.1.call-start
  7.2 1.7 %shard_map.50 = (f32[264,256]{1,0:T(8,128)}, f32[8,64,256]{2,1,0:T(8,128)S(1)}, f32[64,256]{1,0:T(8,128)S(1)}, f32[64,128]{1,0:T(8,128)S(1)}) custom-call(f32[256,256]{1,0:T(8,128)} %rows.1, s32[1,256]{1,0:T(1,128)} %bitcast.29, f32[1,256]{1,0:T(1,128)} %bitcast.22), custom_call_target="tpu_custom_call" | custom-call | tf_op jit(solution)/shard_map/pallas_call | solution.py:300
  8.9 0.0 all-gather.4.cloned.1.call-update
  8.9 0.0 reduce-scatter.2.cloned.1.call-start
  9.0 26.7 %all_to_all.20 = f32[8,64,256]{2,1,0:T(8,128)S(1)} all-to-all(f32[8,64,256]{2,1,0:T(8,128)S(1)} %get-tuple-element.32), channel_id=1, replica_groups=mesh['z'=8,'x'=4,'yh'=4,'yl'=2,'core'=2] {'z'}, dimensions={0} | all-to-all | bytes 1048576 | tf_op jit(solution)/shard_map/all_to_all | solution.py:342
  35.6 0.0 copy-start.1
  35.6 3.1 %collective-permute-start.2 = (f32[512,256]{1,0:T(8,128)S(1)}, f32[512,256]{1,0:T(8,128)S(1)}, u32[]{:S(2)}, u32[]{:S(2)}) collective-permute-start(f32[512,256]{1,0:T(8,128)S(1)} %bitcast.16), channel_id=1, source_target_pairs={{0,16},{16,32},{32,48},{48,0},{1,17},{17,33},{33,49},{49,1},{2,18}... | collective-permute-start | bytes 1572872 | tf_op jit(solution)/shard_map/ppermute | solution.py:323
  38.8 3.4 %collective-permute-start = (f32[512,256]{1,0:T(8,128)S(1)}, f32[512,256]{1,0:T(8,128)S(1)}, u32[]{:S(2)}, u32[]{:S(2)}) collective-permute-start(f32[512,256]{1,0:T(8,128)S(1)} %bitcast.17), channel_id=1, source_target_pairs={{0,48},{16,0},{32,16},{48,32},{1,49},{17,1},{33,17},{49,33},{2,50}... | collective-permute-start | bytes 1572872 | tf_op jit(solution)/shard_map/ppermute | solution.py:323
  42.1 3.4 %collective-permute-start.1 = (f32[512,256]{1,0:T(8,128)S(1)}, f32[512,256]{1,0:T(8,128)S(1)}, u32[]{:S(2)}, u32[]{:S(2)}) collective-permute-start(f32[512,256]{1,0:T(8,128)S(1)} %bitcast.18), channel_id=1, source_target_pairs={{0,32},{16,48},{32,0},{48,16},{1,33},{17,49},{33,1},{49,17},{2,34}... | collective-permute-start | bytes 1572872 | tf_op jit(solution)/shard_map/ppermute | solution.py:323
  45.6 8.1 %all-gather.4.cloned.1.call-done = f32[1056,256]{1,0:T(8,128)} async-done(((f32[264,256]{1,0:T(8,128)}), f32[1056,256]{1,0:T(8,128)}) %all-gather.4.cloned.1.call-update) | async-done | bytes 1081360 | tf_op jit(solution)/shard_map/all_gather | solution.py:343
  53.7 0.0 copy-start
  53.7 1.2 copy-done
  54.9 0.5 shard_map.51
  55.5 3.0 %shard_map.52 = (bf16[1024,512]{1,0:T(8,128)(2,1)}, bf16[1024,512]{1,0:T(8,128)(2,1)}, f32[4,128]{1,0:T(4,128)S(1)}, f32[1024,128]{1,0:T(8,128)S(1)}, f32[1024,256]{1,0:T(8,128)S(1)}) custom-call(bf16[1024,256]{1,0:T(8,128)(2,1)S(1)} %get-tuple-element.30.refs_0_.row_high, bf16[1024,256]{1,0:T(8,128)(2,1)S(1)} %get-tuple-element.31.refs_1_.row_low, ...), custom_call_target="tpu_custom_call" | custom-call | flops 1610612736 | bytes 3670016 | tf_op jit(solution)/shard_map/pallas_call | solution.py:300
  58.5 0.0 copy-done.1
  58.5 0.0 collective-permute-done.2.refs_2_.cols_1.refs_9_
  58.5 0.0 copy-start.2
  58.5 0.0 copy-start.6
  58.5 2.8 %shard_map.53 = (bf16[1024,512]{1,0:T(8,128)(2,1)}, bf16[1024,512]{1,0:T(8,128)(2,1)}, f32[4,128]{1,0:T(4,128)S(1)}, f32[1024,128]{1,0:T(8,128)S(1)}, f32[1024,256]{1,0:T(8,128)S(1)}) custom-call(bf16[1024,256]{1,0:T(8,128)(2,1)S(1)} %get-tuple-element.30.refs_0_.row_high, bf16[1024,256]{1,0:T(8,128)(2,1)S(1)} %get-tuple-element.31.refs_1_.row_low, ...), custom_call_target="tpu_custom_call" | custom-call | flops 1610612736 | bytes 3670016 | tf_op jit(solution)/shard_map/pallas_call | solution.py:300
  61.4 0.0 copy-done.2
  61.4 0.0 collective-permute-done.cols_2.refs_10_
  61.4 0.0 copy-start.3
  61.4 0.5 collective-permute-done.1.cols_3.refs_11_
  61.9 0.0 copy-start.4
  61.9 0.0 copy-done.6
  61.9 6.1 %shard_map.54 = (bf16[1024,512]{1,0:T(8,128)(2,1)}, bf16[1024,512]{1,0:T(8,128)(2,1)}, bf16[1024,512]{1,0:T(8,128)(2,1)}, bf16[1024,512]{1,0:T(8,128)(2,1)}, f32...) custom-call(bf16[1024,256]{1,0:T(8,128)(2,1)S(1)} %get-tuple-element.30.refs_0_.row_high, ...), custom_call_target="tpu_custom_call" | custom-call | flops 3221225472 | bytes 6291456 | tf_op jit(solution)/shard_map/pallas_call | solution.py:300
  68.1 0.0 copy-done.3
  68.1 0.0 copy-done.4
  68.1 0.0 reduce-scatter.2.cloned.1.call-update
  68.1 9.1 %all-to-all-start.1 = ((f32[32,24,128]{2,1,0:T(8,128)}), f32[32,24,128]{2,1,0:T(8,128)S(1)}, u32[]{:S(2)}, u32[]{:S(2)}) async-start(f32[32,24,128]{2,1,0:T(8,128)} %get-tuple-element.41), calls=%async_computation.2 | async-start | bytes 786432 | tf_op jit(solution)/shard_map/all_to_all | solution.py:389
  77.2 5.0 %shard_map.55.refs_12_ = f32[1024,256]{1,0:T(8,128)} custom-call(f32[512,256]{1,0:T(8,128)} %bitcast.20, f32[512,256]{1,0:T(8,128)} %copy-done.2, f32[512,256]{1,0:T(8,128)} %copy-done.3, f32[512,256]{1,0:T(8,128)} %copy-done.4, f32[4,264,256]{2,1,0:T(8,128)} %bitcast.13), custom_call_target="tpu_custom_call" | custom-call | flops 2147483648 | bytes 11534336 | tf_op jit(solution)/shard_map/pallas_call | solution.py:300
  82.2 8.5 %all-to-all-done.1.message = f32[32,24,128]{2,1,0:T(8,128)S(1)} async-done(((f32[32,24,128]{2,1,0:T(8,128)}), f32[32,24,128]{2,1,0:T(8,128)S(1)}, u32[]{:S(2)}, u32[]{:S(2)}) %all-to-all-start.1) | async-done | bytes 393248 | tf_op jit(solution)/shard_map/all_to_all | solution.py:389
  90.8 6.4 %shard_map.56 = (f32[2,4,2,64,256]{4,3,2,1,0:T(8,128)S(1)}, f32[1,128]{1,0:T(1,128)S(1)}) custom-call(f32[32,24,128]{2,1,0:T(8,128)S(1)} %all-to-all-done.1.message, bf16[1024,512]{1,0:T(8,128)(2,1)} %get-tuple-element.42.refs_0_, bf16[1024,512]{1,0:T(8,128)(2,1)} %get-tuple-element.43.refs_1_, bf16[1024,512]{1,0:T(8,128)(2,1)} %get-tuple-element.44.refs_2_, ...), custom_call_target="tpu_custom_call" | custom-call | flops 3221225472 | bytes 11534336 | tf_op jit(solution)/shard_map/pallas_call | solution.py:300
  97.1 7.0 %all_to_all.21 = f32[2,4,2,64,256]{4,3,2,1,0:T(8,128)S(1)} all-to-all(f32[2,4,2,64,256]{4,3,2,1,0:T(8,128)S(1)} %get-tuple-element.52), channel_id=1, replica_groups=mesh['z'=8,'x'=4,'yh'=4,'yl'=2,'core'=2] {'core'}, dimensions={0} | all-to-all | bytes 2097152 | tf_op jit(solution)/shard_map/all_to_all | solution.py:413
  104.1 0.9 reduce_sum.9
  105.0 5.3 %all-to-all-start.3 = ((f32[8,64,256]{2,1,0:T(8,128)}), f32[8,64,256]{2,1,0:T(8,128)S(1)}, u32[]{:S(2)}, u32[]{:S(2)}) async-start(f32[8,64,256]{2,1,0:T(8,128)} %bitcast.7), calls=%async_computation.4 | async-start | bytes 1048576 | tf_op jit(solution)/shard_map/all_to_all | solution.py:414
  110.4 0.0 reduce-scatter.2.cloned.1.call-done.here
  110.4 2.6 %collective-permute-start.3 = (f32[144,256]{1,0:T(8,128)}, f32[144,256]{1,0:T(8,128)S(1)}, u32[]{:S(2)}, u32[]{:S(2)}) collective-permute-start(f32[144,256]{1,0:T(8,128)} %reduce-scatter.2.cloned.1.call-done.here), channel_id=1, source_target_pairs={{0,1},{1,0},{2,3},{3,2},{4,5},{5,4},{6,7},{7,6},{8,9},{9,8},{10,11... | collective-permute-start | bytes 442376 | tf_op jit(solution)/shard_map/ppermute | solution.py:388
  113.0 1.2 collective-permute-done.3.there
  114.2 0.0 copy-start.5
  114.2 0.9 copy-done.5
  115.2 0.2 shard_map.57
  115.4 10.3 %all-gather.1 = f32[32,128]{1,0:T(8,128)S(1)} all-gather(f32[8,128]{1,0:T(8,128)S(1)} %get-tuple-element.51), channel_id=3, replica_groups=mesh['z'=8,'x'=4,'yh'=4,'yl'=2,'core'=2] {'yl','core'}, dimensions={0}, use_global_device_ids=true | all-gather | bytes 20480 | tf_op jit(solution)/shard_map/all_gather | solution.py:421
  125.7 0.6 broadcast_in_dim_reshape_squeeze.3.losses
  126.3 0.6 reshape_squeeze.3
  127.0 1.4 all-to-all-done.3.parts
  128.3 0.1 shard_map.58
  128.5 6.2 %all_gather.19 = f32[256,256]{1,0:T(8,128)S(1)} all-gather(f32[64,256]{1,0:T(8,128)S(1)} %shard_map.58), channel_id=1, replica_groups=mesh['z'=8,'x'=4,'yh'=4,'yl'=2,'core'=2] {'yl','core'}, dimensions={0}, use_global_device_ids=true | all-gather | bytes 327680 | tf_op jit(solution)/shard_map/all_gather | solution.py:429
  134.6 0.7 copy.8
  (1 shorter events, 0.0 us)
Async XLA Ops:
  7.2 46.5 %all-gather.4.cloned.1.call-start = ((), (), s32[]{:S(2)}) async-start(), calls=%async_computation.6 | async-start | bytes 1351680 | tf_op jit(solution)/shard_map/all_gather | solution.py:343
  8.9 101.5 %reduce-scatter.2.cloned.1.call-start = ((), (), s32[]{:S(2)}) async-start(), calls=%async_computation.5 | async-start | bytes 1327104 | tf_op jit(solution)/shard_map/reduce_scatter | solution.py:387
  35.6 22.9 %copy-start.1 = (f32[8,64,256]{2,1,0:T(8,128)}, f32[8,64,256]{2,1,0:T(8,128)S(1)}, u32[]{:S(2)}) copy-start(f32[8,64,256]{2,1,0:T(8,128)S(1)} %all_to_all.20) | copy-start | bytes 1572868
  35.6 22.9 %collective-permute-start.2 = (f32[512,256]{1,0:T(8,128)S(1)}, f32[512,256]{1,0:T(8,128)S(1)}, u32[]{:S(2)}, u32[]{:S(2)}) collective-permute-start(f32[512,256]{1,0:T(8,128)S(1)} %bitcast.16), channel_id=1, source_target_pairs={{0,16},{16,32},{32,48},{48,0},{1,17},{17,33},{33,49},{49,1},{2,18}... | collective-permute-start | bytes 1572872 | tf_op jit(solution)/shard_map/ppermute | solution.py:323
  38.8 22.6 %collective-permute-start = (f32[512,256]{1,0:T(8,128)S(1)}, f32[512,256]{1,0:T(8,128)S(1)}, u32[]{:S(2)}, u32[]{:S(2)}) collective-permute-start(f32[512,256]{1,0:T(8,128)S(1)} %bitcast.17), channel_id=1, source_target_pairs={{0,48},{16,0},{32,16},{48,32},{1,49},{17,1},{33,17},{49,33},{2,50}... | collective-permute-start | bytes 1572872 | tf_op jit(solution)/shard_map/ppermute | solution.py:323
  42.1 19.8 %collective-permute-start.1 = (f32[512,256]{1,0:T(8,128)S(1)}, f32[512,256]{1,0:T(8,128)S(1)}, u32[]{:S(2)}, u32[]{:S(2)}) collective-permute-start(f32[512,256]{1,0:T(8,128)S(1)} %bitcast.18), channel_id=1, source_target_pairs={{0,32},{16,48},{32,0},{48,16},{1,33},{17,49},{33,1},{49,17},{2,34}... | collective-permute-start | bytes 1572872 | tf_op jit(solution)/shard_map/ppermute | solution.py:323
  53.7 1.2 copy-start
  58.5 2.8 %copy-start.2 = (f32[512,256]{1,0:T(8,128)}, f32[512,256]{1,0:T(8,128)S(1)}, u32[]{:S(2)}) copy-start(f32[512,256]{1,0:T(8,128)S(1)} %collective-permute-done.2.refs_2_.cols_1.refs_9_) | copy-start | bytes 1572868
  58.5 3.4 %copy-start.6 = (f32[256]{0:T(256)S(1)}, f32[256]{0:T(256)}, u32[]{:S(2)}) copy-start(f32[256]{0:T(256)} %param.5) | copy-start | bytes 3076
  61.4 6.7 %copy-start.3 = (f32[512,256]{1,0:T(8,128)}, f32[512,256]{1,0:T(8,128)S(1)}, u32[]{:S(2)}) copy-start(f32[512,256]{1,0:T(8,128)S(1)} %collective-permute-done.cols_2.refs_10_) | copy-start | bytes 1572868
  61.9 6.2 %copy-start.4 = (f32[512,256]{1,0:T(8,128)}, f32[512,256]{1,0:T(8,128)S(1)}, u32[]{:S(2)}) copy-start(f32[512,256]{1,0:T(8,128)S(1)} %collective-permute-done.1.cols_3.refs_11_) | copy-start | bytes 1572868
  68.1 22.6 %all-to-all-start.1 = ((f32[32,24,128]{2,1,0:T(8,128)}), f32[32,24,128]{2,1,0:T(8,128)S(1)}, u32[]{:S(2)}, u32[]{:S(2)}) async-start(f32[32,24,128]{2,1,0:T(8,128)} %get-tuple-element.41), calls=%async_computation.2 | async-start | bytes 786432 | tf_op jit(solution)/shard_map/all_to_all | solution.py:389
  105.0 23.3 %all-to-all-start.3 = ((f32[8,64,256]{2,1,0:T(8,128)}), f32[8,64,256]{2,1,0:T(8,128)S(1)}, u32[]{:S(2)}, u32[]{:S(2)}) async-start(f32[8,64,256]{2,1,0:T(8,128)} %bitcast.7), calls=%async_computation.4 | async-start | bytes 1048576 | tf_op jit(solution)/shard_map/all_to_all | solution.py:414
  110.4 3.8 %collective-permute-start.3 = (f32[144,256]{1,0:T(8,128)}, f32[144,256]{1,0:T(8,128)S(1)}, u32[]{:S(2)}, u32[]{:S(2)}) collective-permute-start(f32[144,256]{1,0:T(8,128)} %reduce-scatter.2.cloned.1.call-done.here), channel_id=1, source_target_pairs={{0,1},{1,0},{2,3},{3,2},{4,5},{5,4},{6,7},{7,6},{8,9},{9,8},{10,11... | collective-permute-start | bytes 442376 | tf_op jit(solution)/shard_map/ppermute | solution.py:388
  114.2 0.9 copy-start.5
Sparse Core Ops, SparseCore 0:
  10.1 43.5 all-gather.3
  68.2 38.3 reduce-scatter.1

commit v6 on v5

--- a/solution.py
+++ b/solution.py
@@ -152,35 +152,23 @@
 
 def last_kernel(
     row_high, row_low, cols_2, cols_3, partner, hits, plain, cotangent, sums_0, sums_1, high_2,
-    low_2, high_3, low_3, told, shared_out, *refs,
+    low_2, high_3, low_3, told_out, shared_out, *refs,
 ):
-    *held, sums, shared, sems, shared_sems = refs
+    *held, sums, told, shared, sems, late_sems = refs
     count = cols_2.shape[0]
     outs = (high_2, low_2, high_3, low_3)
     parts = [halves(cols_2[...]), halves(cols_3[...])]
-    copies, totals = [], [None, None]
-    for block in range(row_high.shape[0] // tile):
-        at = slice(block * tile, (block + 1) * tile)
-        summed, hit = plain[at, :], hits[at, :]
+    blocks = [slice(at, at + tile) for at in range(0, row_high.shape[0], tile)]
+    copies, totals, all_hits = [], [None, None], []
+    for block, at in enumerate(blocks):
+        hit = hits[at, :]
         for i in range(2):
             exps, total, more = score(2 + i, at, row_high, row_low, parts[i], partner, count)
             totals[i] = total if block == 0 else totals[i] + total
-            exp_parts = halves(exps)
             ends = slice(2 * i, 2 * i + 2)
-            copies += send_parts(sems.at[block * 2 + i], at, exp_parts, held[ends], outs[ends])
-            summed += products(exp_parts, parts[i])
+            copies += send_parts(sems.at[block * 2 + i], at, halves(exps), held[ends], outs[ends])
             hit += more
-        for part in range(tile // lanes):
-            turned = jnp.transpose(hit[part * lanes : (part + 1) * lanes, :])
-            row = math.log(2.0) * jnp.sum(turned, axis=0, keepdims=True)
-            for side in range(2):
-                k = block * 4 + part * 2 + side
-                shared[k, :quarter, :] = summed[(part * 2 + side) * 64 : (part * 2 + side + 1) * 64]
-                shared[k, quarter:, :] = jnp.zeros((8, shared.shape[2]), f32)
-                here = row if side == 0 else pltpu.roll(row, 64, 1)
-                shared[k, quarter : quarter + 1, :lanes] = here
-        ends = pl.ds(block * 4, 4)
-        copies += fetch(shared_sems.at[block], (shared.at[ends], shared_out.at[ends]))
+        all_hits.append(hit)
     own = cotangent[pl.ds(lax.axis_index("yl"), 1), :]
     own = jnp.where(lax.axis_index("core") == 0, own, pltpu.roll(own, 64, 1))
     late = [jnp.concatenate(pieces(total), axis=0) for total in totals]
@@ -190,6 +178,22 @@
     sums[16:17, :] = own
     sums[17:, :] = jnp.zeros((7, lanes), f32)
     told[...] = jnp.broadcast_to(sums[...][None], told.shape)
+    copies += fetch(late_sems.at[4], (told, told_out))
+    for block, at in enumerate(blocks):
+        summed = plain[at, :]
+        for i in range(2):
+            summed += products((held[2 * i][at, :], held[2 * i + 1][at, :]), parts[i])
+        for part in range(tile // lanes):
+            turned = jnp.transpose(all_hits[block][part * lanes : (part + 1) * lanes, :])
+            row = math.log(2.0) * jnp.sum(turned, axis=0, keepdims=True)
+            for side in range(2):
+                k = block * 4 + part * 2 + side
+                shared[k, :quarter, :] = summed[(part * 2 + side) * 64 : (part * 2 + side + 1) * 64]
+                shared[k, quarter:, :] = jnp.zeros((8, shared.shape[2]), f32)
+                here = row if side == 0 else pltpu.roll(row, 64, 1)
+                shared[k, quarter : quarter + 1, :lanes] = here
+        ends = pl.ds(block * 4, 4)
+        copies += fetch(late_sems.at[block], (shared.at[ends], shared_out.at[ends]))
     wait_all(copies)
 
 
@@ -378,9 +382,9 @@
         32,
         estimate(6, count, 2 * seen, width, 2 * count * seen),
         own_exps * 2
-        + [pltpu.VMEM((24, lanes), f32), pltpu.VMEM((16, quarter + 8, width), f32)]
-        + [copies((8, 2)), copies((4, 1))],
-        far_outs=(0, 1, 2, 3, 5),
+        + [pltpu.VMEM((24, lanes), f32), pltpu.VMEM((32, 24, lanes), f32)]
+        + [pltpu.VMEM((16, quarter + 8, width), f32), copies((8, 2)), copies((5, 1))],
+        far_outs=range(6),
     )
     highs += [high_2, high_3]
     lows += [low_2, low_3]

time: 143 us -> 141 us (0.986)
  no operation moved by 1% of the time
where the time goes in v6:
time: 141 us
  blocking collectives  50.2 us (36%)
  starting transfers between devices  27 us (19%)
  Pallas kernels  24.5 us (17%)
  waiting for transfers between devices  19.8 us (14%)
  between operations  14.2 us (10%)
  local copies, waits for them, and re-layouts  4.16 us (3%)
    all_to_all x1, blocking collectives, per_device(): here = lax.all_to_all(told, 'z', 0, 0, tiled=True).reshape(seen, width)  26.7 us
    pallas_call x9, Pallas kernels, call(): pl.pallas_call(kernel, in_specs=[anywhere if i in far else vmem for i in...  24.5 us
    all_gather x1, blocking collectives, per_device(): losses = lax.all_gather(losses, ('yl', 'core'))[:, 0, :quarter].reshape(-1)  10.4 us
    ppermute x3, starting transfers between devices, passed_along(): return lax.ppermute(array, 'x', [(i, (i + by) % 4) for i in range(4)])  9.92 us
    all_to_all x1, starting transfers between devices, per_device(): message = lax.all_to_all(told, ('z', 'x'), 0, 0, tiled=True)  9.13 us
    all_to_all x1, waiting for transfers between devices, per_device(): message = lax.all_to_all(told, ('z', 'x'), 0, 0, tiled=True)  8.51 us
    all_gather x1, waiting for transfers between devices, per_device(): rows = lax.all_gather(packed_rows, 'yh')  8.11 us
    all_to_all x1, blocking collectives, per_device(): halved = jnp.sum(lax.all_to_all(partial, 'core', 0, 0, tiled=True), axis=0)  6.98 us
  transfers between devices with their start and end apart: 8, of which 5 were waited for; matrix products, arithmetic and copies ran while one was open for 2% of the time, Pallas kernels for 13%

profile of v6, /device:TPU:1, one launch (start us, length us, event | category | flops | bytes accessed | tf_op | source)
XLA Modules:
  0.0 140.8 jit_solution(1802872165695450837)
XLA Ops:
  7.2 0.0 all-gather.4.cloned.1.call-start
  7.2 1.7 %shard_map.50 = (f32[264,256]{1,0:T(8,128)}, f32[8,64,256]{2,1,0:T(8,128)S(1)}, f32[64,256]{1,0:T(8,128)S(1)}, f32[64,128]{1,0:T(8,128)S(1)}) custom-call(f32[256,256]{1,0:T(8,128)} %rows.1, s32[1,256]{1,0:T(1,128)} %bitcast.29, f32[1,256]{1,0:T(1,128)} %bitcast.22), custom_call_target="tpu_custom_call" | custom-call | tf_op jit(solution)/shard_map/pallas_call | solution.py:304
  8.9 0.0 all-gather.4.cloned.1.call-update
  8.9 0.0 reduce-scatter.2.cloned.1.call-start
  9.0 26.7 %all_to_all.20 = f32[8,64,256]{2,1,0:T(8,128)S(1)} all-to-all(f32[8,64,256]{2,1,0:T(8,128)S(1)} %get-tuple-element.32), channel_id=1, replica_groups=mesh['z'=8,'x'=4,'yh'=4,'yl'=2,'core'=2] {'z'}, dimensions={0} | all-to-all | bytes 1048576 | tf_op jit(solution)/shard_map/all_to_all | solution.py:346
  35.6 0.0 copy-start.1
  35.6 3.1 %collective-permute-start.2 = (f32[512,256]{1,0:T(8,128)S(1)}, f32[512,256]{1,0:T(8,128)S(1)}, u32[]{:S(2)}, u32[]{:S(2)}) collective-permute-start(f32[512,256]{1,0:T(8,128)S(1)} %bitcast.16), channel_id=1, source_target_pairs={{0,16},{16,32},{32,48},{48,0},{1,17},{17,33},{33,49},{49,1},{2,18}... | collective-permute-start | bytes 1572872 | tf_op jit(solution)/shard_map/ppermute | solution.py:327
  38.8 3.4 %collective-permute-start = (f32[512,256]{1,0:T(8,128)S(1)}, f32[512,256]{1,0:T(8,128)S(1)}, u32[]{:S(2)}, u32[]{:S(2)}) collective-permute-start(f32[512,256]{1,0:T(8,128)S(1)} %bitcast.17), channel_id=1, source_target_pairs={{0,48},{16,0},{32,16},{48,32},{1,49},{17,1},{33,17},{49,33},{2,50}... | collective-permute-start | bytes 1572872 | tf_op jit(solution)/shard_map/ppermute | solution.py:327
  42.1 3.4 %collective-permute-start.1 = (f32[512,256]{1,0:T(8,128)S(1)}, f32[512,256]{1,0:T(8,128)S(1)}, u32[]{:S(2)}, u32[]{:S(2)}) collective-permute-start(f32[512,256]{1,0:T(8,128)S(1)} %bitcast.18), channel_id=1, source_target_pairs={{0,32},{16,48},{32,0},{48,16},{1,33},{17,49},{33,1},{49,17},{2,34}... | collective-permute-start | bytes 1572872 | tf_op jit(solution)/shard_map/ppermute | solution.py:327
  45.6 8.1 %all-gather.4.cloned.1.call-done = f32[1056,256]{1,0:T(8,128)} async-done(((f32[264,256]{1,0:T(8,128)}), f32[1056,256]{1,0:T(8,128)}) %all-gather.4.cloned.1.call-update) | async-done | bytes 1081360 | tf_op jit(solution)/shard_map/all_gather | solution.py:347
  53.7 0.0 copy-start
  53.7 1.2 copy-done
  54.9 0.5 shard_map.51
  55.5 3.0 %shard_map.52 = (bf16[1024,512]{1,0:T(8,128)(2,1)}, bf16[1024,512]{1,0:T(8,128)(2,1)}, f32[4,128]{1,0:T(4,128)S(1)}, f32[1024,128]{1,0:T(8,128)S(1)}, f32[1024,256]{1,0:T(8,128)S(1)}) custom-call(bf16[1024,256]{1,0:T(8,128)(2,1)S(1)} %get-tuple-element.30.refs_0_.row_high, bf16[1024,256]{1,0:T(8,128)(2,1)S(1)} %get-tuple-element.31.refs_1_.row_low, ...), custom_call_target="tpu_custom_call" | custom-call | flops 1610612736 | bytes 3670016 | tf_op jit(solution)/shard_map/pallas_call | solution.py:304
  58.5 0.0 copy-done.1
  58.5 0.0 collective-permute-done.2.refs_2_.cols_1.refs_9_
  58.5 0.0 copy-start.2
  58.5 0.0 copy-start.6
  58.5 2.8 %shard_map.53 = (bf16[1024,512]{1,0:T(8,128)(2,1)}, bf16[1024,512]{1,0:T(8,128)(2,1)}, f32[4,128]{1,0:T(4,128)S(1)}, f32[1024,128]{1,0:T(8,128)S(1)}, f32[1024,256]{1,0:T(8,128)S(1)}) custom-call(bf16[1024,256]{1,0:T(8,128)(2,1)S(1)} %get-tuple-element.30.refs_0_.row_high, bf16[1024,256]{1,0:T(8,128)(2,1)S(1)} %get-tuple-element.31.refs_1_.row_low, ...), custom_call_target="tpu_custom_call" | custom-call | flops 1610612736 | bytes 3670016 | tf_op jit(solution)/shard_map/pallas_call | solution.py:304
  61.4 0.0 copy-done.2
  61.4 0.0 collective-permute-done.cols_2.refs_10_
  61.4 0.0 copy-start.3
  61.4 0.5 collective-permute-done.1.cols_3.refs_11_
  61.9 0.0 copy-start.4
  61.9 0.0 copy-done.6
  61.9 4.8 %shard_map.54 = (bf16[1024,512]{1,0:T(8,128)(2,1)}, bf16[1024,512]{1,0:T(8,128)(2,1)}, bf16[1024,512]{1,0:T(8,128)(2,1)}, bf16[1024,512]{1,0:T(8,128)(2,1)}, f32...) custom-call(bf16[1024,256]{1,0:T(8,128)(2,1)S(1)} %get-tuple-element.30.refs_0_.row_high, ...), custom_call_target="tpu_custom_call" | custom-call | flops 3221225472 | bytes 6291456 | tf_op jit(solution)/shard_map/pallas_call | solution.py:304
  66.7 0.0 copy-done.3
  66.7 0.0 copy-done.4
  66.7 0.0 reduce-scatter.2.cloned.1.call-update
  66.7 9.1 %all-to-all-start.1 = ((f32[32,24,128]{2,1,0:T(8,128)}), f32[32,24,128]{2,1,0:T(8,128)S(1)}, u32[]{:S(2)}, u32[]{:S(2)}) async-start(f32[32,24,128]{2,1,0:T(8,128)} %get-tuple-element.41), calls=%async_computation.2 | async-start | bytes 786432 | tf_op jit(solution)/shard_map/all_to_all | solution.py:393
  75.9 5.0 %shard_map.55.refs_12_ = f32[1024,256]{1,0:T(8,128)} custom-call(f32[512,256]{1,0:T(8,128)} %bitcast.20, f32[512,256]{1,0:T(8,128)} %copy-done.2, f32[512,256]{1,0:T(8,128)} %copy-done.3, f32[512,256]{1,0:T(8,128)} %copy-done.4, f32[4,264,256]{2,1,0:T(8,128)} %bitcast.13), custom_call_target="tpu_custom_call" | custom-call | flops 2147483648 | bytes 11534336 | tf_op jit(solution)/shard_map/pallas_call | solution.py:304
  80.8 8.5 %all-to-all-done.1.message = f32[32,24,128]{2,1,0:T(8,128)S(1)} async-done(((f32[32,24,128]{2,1,0:T(8,128)}), f32[32,24,128]{2,1,0:T(8,128)S(1)}, u32[]{:S(2)}, u32[]{:S(2)}) %all-to-all-start.1) | async-done | bytes 393248 | tf_op jit(solution)/shard_map/all_to_all | solution.py:393
  89.4 6.4 %shard_map.56 = (f32[2,4,2,64,256]{4,3,2,1,0:T(8,128)S(1)}, f32[1,128]{1,0:T(1,128)S(1)}) custom-call(f32[32,24,128]{2,1,0:T(8,128)S(1)} %all-to-all-done.1.message, bf16[1024,512]{1,0:T(8,128)(2,1)} %get-tuple-element.42.refs_0_, bf16[1024,512]{1,0:T(8,128)(2,1)} %get-tuple-element.43.refs_1_, bf16[1024,512]{1,0:T(8,128)(2,1)} %get-tuple-element.44.refs_2_, ...), custom_call_target="tpu_custom_call" | custom-call | flops 3221225472 | bytes 11534336 | tf_op jit(solution)/shard_map/pallas_call | solution.py:304
  95.7 7.0 %all_to_all.21 = f32[2,4,2,64,256]{4,3,2,1,0:T(8,128)S(1)} all-to-all(f32[2,4,2,64,256]{4,3,2,1,0:T(8,128)S(1)} %get-tuple-element.52), channel_id=1, replica_groups=mesh['z'=8,'x'=4,'yh'=4,'yl'=2,'core'=2] {'core'}, dimensions={0} | all-to-all | bytes 2097152 | tf_op jit(solution)/shard_map/all_to_all | solution.py:417
  102.7 0.9 reduce_sum.9
  103.7 5.3 %all-to-all-start.3 = ((f32[8,64,256]{2,1,0:T(8,128)}), f32[8,64,256]{2,1,0:T(8,128)S(1)}, u32[]{:S(2)}, u32[]{:S(2)}) async-start(f32[8,64,256]{2,1,0:T(8,128)} %bitcast.7), calls=%async_computation.4 | async-start | bytes 1048576 | tf_op jit(solution)/shard_map/all_to_all | solution.py:418
  109.0 0.0 reduce-scatter.2.cloned.1.call-done.here
  109.0 2.6 %collective-permute-start.3 = (f32[144,256]{1,0:T(8,128)}, f32[144,256]{1,0:T(8,128)S(1)}, u32[]{:S(2)}, u32[]{:S(2)}) collective-permute-start(f32[144,256]{1,0:T(8,128)} %reduce-scatter.2.cloned.1.call-done.here), channel_id=1, source_target_pairs={{0,1},{1,0},{2,3},{3,2},{4,5},{5,4},{6,7},{7,6},{8,9},{9,8},{10,11... | collective-permute-start | bytes 442376 | tf_op jit(solution)/shard_map/ppermute | solution.py:392
  111.6 1.2 collective-permute-done.3.there
  112.8 0.0 copy-start.5
  112.8 0.9 copy-done.5
  113.7 0.2 shard_map.57
  113.9 10.4 %all-gather.1 = f32[32,128]{1,0:T(8,128)S(1)} all-gather(f32[8,128]{1,0:T(8,128)S(1)} %get-tuple-element.51), channel_id=3, replica_groups=mesh['z'=8,'x'=4,'yh'=4,'yl'=2,'core'=2] {'yl','core'}, dimensions={0}, use_global_device_ids=true | all-gather | bytes 20480 | tf_op jit(solution)/shard_map/all_gather | solution.py:425
  124.3 0.6 broadcast_in_dim_reshape_squeeze.3.losses
  124.9 0.6 reshape_squeeze.3
  125.6 1.4 all-to-all-done.3.parts
  127.0 0.1 shard_map.58
  127.1 6.2 %all_gather.19 = f32[256,256]{1,0:T(8,128)S(1)} all-gather(f32[64,256]{1,0:T(8,128)S(1)} %shard_map.58), channel_id=1, replica_groups=mesh['z'=8,'x'=4,'yh'=4,'yl'=2,'core'=2] {'yl','core'}, dimensions={0}, use_global_device_ids=true | all-gather | bytes 327680 | tf_op jit(solution)/shard_map/all_gather | solution.py:433
  133.3 0.7 copy.8
  (1 shorter events, 0.0 us)
Async XLA Ops:
  7.2 46.5 %all-gather.4.cloned.1.call-start = ((), (), s32[]{:S(2)}) async-start(), calls=%async_computation.6 | async-start | bytes 1351680 | tf_op jit(solution)/shard_map/all_gather | solution.py:347
  8.9 100.1 %reduce-scatter.2.cloned.1.call-start = ((), (), s32[]{:S(2)}) async-start(), calls=%async_computation.5 | async-start | bytes 1327104 | tf_op jit(solution)/shard_map/reduce_scatter | solution.py:391
  35.6 22.9 %copy-start.1 = (f32[8,64,256]{2,1,0:T(8,128)}, f32[8,64,256]{2,1,0:T(8,128)S(1)}, u32[]{:S(2)}) copy-start(f32[8,64,256]{2,1,0:T(8,128)S(1)} %all_to_all.20) | copy-start | bytes 1572868
  35.6 22.9 %collective-permute-start.2 = (f32[512,256]{1,0:T(8,128)S(1)}, f32[512,256]{1,0:T(8,128)S(1)}, u32[]{:S(2)}, u32[]{:S(2)}) collective-permute-start(f32[512,256]{1,0:T(8,128)S(1)} %bitcast.16), channel_id=1, source_target_pairs={{0,16},{16,32},{32,48},{48,0},{1,17},{17,33},{33,49},{49,1},{2,18}... | collective-permute-start | bytes 1572872 | tf_op jit(solution)/shard_map/ppermute | solution.py:327
  38.8 22.6 %collective-permute-start = (f32[512,256]{1,0:T(8,128)S(1)}, f32[512,256]{1,0:T(8,128)S(1)}, u32[]{:S(2)}, u32[]{:S(2)}) collective-permute-start(f32[512,256]{1,0:T(8,128)S(1)} %bitcast.17), channel_id=1, source_target_pairs={{0,48},{16,0},{32,16},{48,32},{1,49},{17,1},{33,17},{49,33},{2,50}... | collective-permute-start | bytes 1572872 | tf_op jit(solution)/shard_map/ppermute | solution.py:327
  42.1 19.8 %collective-permute-start.1 = (f32[512,256]{1,0:T(8,128)S(1)}, f32[512,256]{1,0:T(8,128)S(1)}, u32[]{:S(2)}, u32[]{:S(2)}) collective-permute-start(f32[512,256]{1,0:T(8,128)S(1)} %bitcast.18), channel_id=1, source_target_pairs={{0,32},{16,48},{32,0},{48,16},{1,33},{17,49},{33,1},{49,17},{2,34}... | collective-permute-start | bytes 1572872 | tf_op jit(solution)/shard_map/ppermute | solution.py:327
  53.7 1.2 copy-start
  58.5 2.8 %copy-start.2 = (f32[512,256]{1,0:T(8,128)}, f32[512,256]{1,0:T(8,128)S(1)}, u32[]{:S(2)}) copy-start(f32[512,256]{1,0:T(8,128)S(1)} %collective-permute-done.2.refs_2_.cols_1.refs_9_) | copy-start | bytes 1572868
  58.5 3.4 %copy-start.6 = (f32[256]{0:T(256)S(1)}, f32[256]{0:T(256)}, u32[]{:S(2)}) copy-start(f32[256]{0:T(256)} %param.5) | copy-start | bytes 3076
  61.4 5.3 %copy-start.3 = (f32[512,256]{1,0:T(8,128)}, f32[512,256]{1,0:T(8,128)S(1)}, u32[]{:S(2)}) copy-start(f32[512,256]{1,0:T(8,128)S(1)} %collective-permute-done.cols_2.refs_10_) | copy-start | bytes 1572868
  61.9 4.8 %copy-start.4 = (f32[512,256]{1,0:T(8,128)}, f32[512,256]{1,0:T(8,128)S(1)}, u32[]{:S(2)}) copy-start(f32[512,256]{1,0:T(8,128)S(1)} %collective-permute-done.1.cols_3.refs_11_) | copy-start | bytes 1572868
  66.7 22.6 %all-to-all-start.1 = ((f32[32,24,128]{2,1,0:T(8,128)}), f32[32,24,128]{2,1,0:T(8,128)S(1)}, u32[]{:S(2)}, u32[]{:S(2)}) async-start(f32[32,24,128]{2,1,0:T(8,128)} %get-tuple-element.41), calls=%async_computation.2 | async-start | bytes 786432 | tf_op jit(solution)/shard_map/all_to_all | solution.py:393
  103.7 23.3 %all-to-all-start.3 = ((f32[8,64,256]{2,1,0:T(8,128)}), f32[8,64,256]{2,1,0:T(8,128)S(1)}, u32[]{:S(2)}, u32[]{:S(2)}) async-start(f32[8,64,256]{2,1,0:T(8,128)} %bitcast.7), calls=%async_computation.4 | async-start | bytes 1048576 | tf_op jit(solution)/shard_map/all_to_all | solution.py:418
  109.0 3.8 %collective-permute-start.3 = (f32[144,256]{1,0:T(8,128)}, f32[144,256]{1,0:T(8,128)S(1)}, u32[]{:S(2)}, u32[]{:S(2)}) collective-permute-start(f32[144,256]{1,0:T(8,128)} %reduce-scatter.2.cloned.1.call-done.here), channel_id=1, source_target_pairs={{0,1},{1,0},{2,3},{3,2},{4,5},{5,4},{6,7},{7,6},{8,9},{9,8},{10,11... | collective-permute-start | bytes 442376 | tf_op jit(solution)/shard_map/ppermute | solution.py:392
  112.8 0.9 copy-start.5
Sparse Core Ops, SparseCore 0:
  10.1 43.5 all-gather.3
  66.8 38.3 reduce-scatter.1
